TPU v7x, 32 devices: a whole 2x2x4 slice. The times are simulated.
32 devices in a mesh: gx: 4 (over z), gy: 8 (over y, x, core).
Axes of the slice: x: 2, y: 2, z: 4, core: 2. Of those that a mesh axis runs over, the one named last changes fastest.
Arguments:
- objective_grad: bfloat16 [64, 2048, 128], P('gx', 'gy'), may hold values from -6 to 6
- adjoint_start: bfloat16 [64, 2048, 128], P('gx', 'gy'), may hold values from -6 to 6
- levels: int32 [64, 2048], P('gx', 'gy'), may hold values from 1 to 16
- stiffness: bfloat16 [9, 64, 64], replicated
- row_cells: int32 [131072], P(('gx', 'gy')), may hold values from 0 to 4095
- row_front: int32 [131072, 1], P(('gx', 'gy')), may hold values from 0 to 63; in each aligned block of 4096 rows (0 to 4095, 4096 to 8191, ...) at most 128 rows name the same one
- row_pos: int32 [131072], P(('gx', 'gy')), may hold values from 0 to 511
- front_place: int32 [64], replicated, may hold values from 0 to 63, each once
- schur: bfloat16 [64, 512, 512], P(('gx', 'gy')), may hold values from -0.25 to 0.25
Outputs:
- adjoint: float32 [64, 2048, 128], P('gx', 'gy')
- front_values: float32 [64, 512, 128], P(('gx', 'gy'))
Inputs may be any that keep to these rules, and one draw needn't show every extreme that they name: `row_cells`: a segment of the listing subdomain's 16 x 256 block, counted row-major. `row_front`: among the rows of one subdomain at most 128 name the same front, a bound that some block reaches of them. `front_place`: each place is taken once; place q is held by device q // 2 in the order gx 8 + gy.
All inputs are finite; a program needn't handle non-finite values.
Results may differ from a plain program's by a relative error of at most 0.0042.
Values may be sent and summed in bfloat16 or wider, within the bound.
A program may use at most 128 MiB of HBM per device.

v0:
```python
import jax
import jax.numpy as jnp
from jax import lax
from jax.sharding import PartitionSpec as P

LEVELS = 16


soft_floor = 0.001
relax_rate = 0.5


def extended(value, sides, width):
    for axis, dim in sides:
        size, length = (lax.axis_size(axis), value.shape[dim])
        up = [(i, (i + 1) % size) for i in range(size - 1)]
        down = [(j, i) for i, j in up]
        last = lax.slice_in_dim(value, length - width, length, axis=dim)
        leading = lax.slice_in_dim(value, 0, width, axis=dim)
        before = lax.ppermute(last, axis, up)
        after = lax.ppermute(leading, axis, down)
        value = jnp.concatenate([before, value, after], axis=dim)
    return value


def cell_weight(levels):
    ratio = levels.astype(jnp.float32) / LEVELS
    return soft_floor + (1.0 - soft_floor) * ratio * ratio * ratio


def stiffness_apply(padded, stiffness, out_rows, out_cols):
    summed = jnp.zeros((out_rows, out_cols, padded.shape[2]), jnp.float32)
    for shift_row in (-1, 0, 1):
        for shift_col in (-1, 0, 1):
            source = padded[
                1 - shift_row : 1 - shift_row + out_rows,
                1 - shift_col : 1 - shift_col + out_cols,
                :,
            ]
            flattened = source.reshape(-1, stiffness.shape[1])
            product = jnp.dot(
                flattened,
                stiffness[3 * (shift_row + 1) + (shift_col + 1)],
                preferred_element_type=jnp.float32,
            )
            summed = summed + product.reshape(out_rows, out_cols, -1)
    return summed


def local(
    objective_grad,
    adjoint_start,
    levels,
    stiffness,
    row_cells,
    row_front,
    row_pos,
    front_place,
    schur,
):
    block_rows, block_cols, row_width = objective_grad.shape
    weight = cell_weight(levels)
    grad_local = objective_grad.astype(jnp.float32)
    adjoint_now = adjoint_start.astype(jnp.float32)
    for sweep in range(3):
        scaled = (weight[:, :, None] * adjoint_now).astype(jnp.bfloat16)
        padded = extended(scaled, (("gx", 0), ("gy", 1)), 1)
        image = stiffness_apply(padded, stiffness, block_rows, block_cols)
        adjoint_now = adjoint_now + relax_rate * (grad_local - image)
    sent_field = adjoint_now.astype(jnp.bfloat16).reshape(block_rows * block_cols, row_width)
    picked = jnp.take(sent_field, row_cells, axis=0)
    fronts = row_front[:, 0]
    front_count = front_place.shape[0]
    member = (fronts[:, None] == jnp.arange(front_count, dtype=jnp.int32)[None, :]).astype(
        jnp.int32
    )
    places = jnp.sum(member * front_place[None, :], axis=1)
    ranks = jnp.sum((jnp.cumsum(member, axis=0) - member) * member, axis=1)
    owned = schur.shape[0]
    capacity = 2 * row_cells.shape[0] // front_count
    slot_total = owned * capacity
    grid_x = lax.axis_size("gx")
    grid_y = lax.axis_size("gy")
    devices = grid_x * grid_y
    targets = places // owned * slot_total + places % owned * capacity + ranks
    buffer = jnp.zeros((devices * slot_total, row_width), jnp.bfloat16).at[targets].set(picked)
    spots = jnp.full((devices * slot_total,), -1, jnp.int32).at[targets].set(row_pos)
    rows_in, spots_in = (
        lax.all_to_all(
            buffer.reshape(devices, slot_total, row_width),
            ("gx", "gy"),
            split_axis=0,
            concat_axis=0,
            tiled=True,
        ),
        lax.all_to_all(
            spots.reshape(devices, slot_total),
            ("gx", "gy"),
            split_axis=0,
            concat_axis=0,
            tiled=True,
        ),
    )
    rows_in = rows_in.reshape(devices, owned, capacity, row_width)
    spots_in = spots_in.reshape(devices, owned, capacity)
    front_size = schur.shape[1]
    results = []
    for slot in range(owned):
        slot_rows = rows_in[:, slot].reshape(devices * capacity, row_width)
        slot_spots = spots_in[:, slot].reshape(devices * capacity)
        selector = (jnp.arange(front_size, dtype=jnp.int32)[:, None] == slot_spots[None, :]).astype(
            jnp.bfloat16
        )
        assembled = jnp.dot(selector, slot_rows, preferred_element_type=jnp.float32).astype(
            jnp.bfloat16
        )
        results.append(jnp.dot(schur[slot], assembled, preferred_element_type=jnp.float32))
    return (adjoint_now, jnp.stack(results))


def solution(mesh):
    placed = (
        P("gx", "gy", None),
        P("gx", "gy", None),
        P("gx", "gy"),
        P(),
        P(("gx", "gy")),
        P(("gx", "gy"), None),
        P(("gx", "gy")),
        P(),
        P(("gx", "gy"), None, None),
    )
    return jax.shard_map(
        local,
        mesh=mesh,
        in_specs=placed,
        out_specs=(P("gx", "gy", None), P(("gx", "gy"), None, None)),
        check_vma=False,
    )
```

profile of v0, /device:TPU:0, one launch (start us, length us, event | category | flops | bytes accessed | tf_op | source)
XLA Modules:
  0.0 380.5 jit_solution(4518275672512116960)
XLA Ops:
  3.8 4.9 %collective-permute-start = (bf16[1,256,128]{2,1,0:T(8,128)(2,1)}, bf16[1,256,128]{2,1,0:T(8,128)(2,1)S(1)}, u32[]{:S(2)}, u32[]{:S(2)}) collective-permute-start(bf16[1,256,128]{2,1,0:T(8,128)(2,1)} %get-tuple-element.52), channel_id=1, source_target_pairs={{0,8},{8,16},{16,24},{1,9},{9,17},{17,25},{2,10},{10,18},{18,26},{... | collective-permute-start | bytes 196616 | tf_op jit(solution)/shard_map/ppermute | solution.py:20
  10.1 18.4 %reduce-window.6 = s32[64,32,128]{2,1,0:T(8,128)S(1)} reduce-window(s32[64,32,128]{2,1,0:T(8,128)S(1)} %fusion.22, s32[]{:T(128)} %constant.57.clone.1), window={size=1x1x128 pad=0_0x0_0x127_0}, to_apply=%region_1.2 | reduce-window | flops 33292288 | bytes 2097156 | tf_op jit(solution)/shard_map/reduce-window
  31.1 16.3 %scatter_custom_fusion = s32[8192]{0:T(1024)} fusion(s32[4096]{0:T(1024)S(1)} %bitcast.152, s32[4096]{0:T(1024)} %param.15, s32[]{:T(128)} %constant.56.clone.1), kind=kCustom, calls=%fused_computation.126 | custom fusion | bytes 33280 | tf_op jit(solution)/shard_map/scatter | solution.py:87
  47.4 6.9 %all-to-all-start = ((s32[32,1,256]{2,1,0:T(1,128)}), s32[32,1,256]{2,1,0:T(1,128)S(1)}, u32[]{:S(2)}, u32[]{:S(2)}) async-start(s32[32,1,256]{2,1,0:T(1,128)} %bitcast.17), calls=%async_computation | async-start | bytes 65536 | tf_op jit(solution)/shard_map/all_to_all | solution.py:96
  56.5 3.2 collective-permute-start.3
  61.2 3.9 %reshape.284 = bf16[8192,64]{1,0:T(8,128)(2,1)} reshape(bf16[16,256,128]{2,1,0:T(8,128)(2,1)} %get-tuple-element.51) | data formatting | bytes 2097152 | tf_op jit(solution)/shard_map/reshape | solution.py:40
  65.1 3.8 %fusion.60 = f32[8192,64]{0,1:T(8,128)} fusion(bf16[8192,64]{1,0:T(8,128)(2,1)} %reshape.284, bf16[9,64,64]{2,1,0:T(8,128)(2,1)S(1)} %copy-done.30), kind=kOutput, calls=%fused_computation.121 | convolution fusion | flops 67108864 | bytes 3162112 | tf_op jit(solution)/shard_map/dot_general | solution.py:41
  68.9 3.8 %reshape.292 = bf16[8192,64]{1,0:T(8,128)(2,1)} reshape(bf16[16,256,128]{2,1,0:T(8,128)(2,1)} %get-tuple-element.50) | data formatting | bytes 2097152 | tf_op jit(solution)/shard_map/reshape | solution.py:40
  73.4 2.7 fusion.103
  76.1 3.8 %reshape.283 = bf16[8192,64]{1,0:T(8,128)(2,1)} reshape(bf16[16,256,128]{2,1,0:T(8,128)(2,1)} %get-tuple-element.26) | data formatting | bytes 2097152 | tf_op jit(solution)/shard_map/reshape | solution.py:40
  79.9 3.9 %reshape.285 = bf16[8192,64]{1,0:T(8,128)(2,1)} reshape(bf16[16,256,128]{2,1,0:T(8,128)(2,1)} %get-tuple-element.56) | data formatting | bytes 2097152 | tf_op jit(solution)/shard_map/reshape | solution.py:40
  83.8 3.8 %reshape.286 = bf16[8192,64]{1,0:T(8,128)(2,1)} reshape(bf16[16,256,128]{2,1,0:T(8,128)(2,1)} %get-tuple-element.25) | data formatting | bytes 2097152 | tf_op jit(solution)/shard_map/reshape | solution.py:40
  87.7 3.9 %reshape.288 = bf16[8192,64]{1,0:T(8,128)(2,1)} reshape(bf16[16,256,128]{2,1,0:T(8,128)(2,1)} %get-tuple-element.58) | data formatting | bytes 2097152 | tf_op jit(solution)/shard_map/reshape | solution.py:40
  91.6 3.8 %reshape.290 = bf16[8192,64]{1,0:T(8,128)(2,1)} reshape(bf16[16,256,128]{2,1,0:T(8,128)(2,1)} %get-tuple-element.24) | data formatting | bytes 2097152 | tf_op jit(solution)/shard_map/reshape | solution.py:40
  97.3 2.6 fusion.36
  109.8 2.8 copy.12
  112.6 3.3 reshape.336
  118.5 3.7 collective-permute-start.4
  125.3 3.8 collective-permute-done.5
  130.5 3.8 %reshape.297 = bf16[8192,64]{1,0:T(8,128)(2,1)} reshape(bf16[16,256,128]{2,1,0:T(8,128)(2,1)} %get-tuple-element.47) | data formatting | bytes 2097152 | tf_op jit(solution)/shard_map/reshape | solution.py:40
  135.7 3.0 collective-permute-start.7
  138.7 3.8 %fusion.58 = f32[8192,64]{0,1:T(8,128)} fusion(bf16[8192,64]{1,0:T(8,128)(2,1)} %reshape.297, bf16[9,64,64]{2,1,0:T(8,128)(2,1)S(1)} %copy-done.30), kind=kOutput, calls=%fused_computation.119 | convolution fusion | flops 67108864 | bytes 3162112 | tf_op jit(solution)/shard_map/dot_general | solution.py:41
  142.5 4.2 %reshape.305 = bf16[8192,64]{1,0:T(8,128)(2,1)} reshape(bf16[16,256,128]{2,1,0:T(8,128)(2,1)} %get-tuple-element.46) | data formatting | bytes 2097152 | tf_op jit(solution)/shard_map/reshape | solution.py:40
  150.6 4.0 %reshape.296 = bf16[8192,64]{1,0:T(8,128)(2,1)} reshape(bf16[16,256,128]{2,1,0:T(8,128)(2,1)} %get-tuple-element.20) | data formatting | bytes 2097152 | tf_op jit(solution)/shard_map/reshape | solution.py:40
  156.5 3.9 %reshape.298 = bf16[8192,64]{1,0:T(8,128)(2,1)} reshape(bf16[16,256,128]{2,1,0:T(8,128)(2,1)} %get-tuple-element.23) | data formatting | bytes 2097152 | tf_op jit(solution)/shard_map/reshape | solution.py:40
  162.2 4.0 %reshape.301 = bf16[8192,64]{1,0:T(8,128)(2,1)} reshape(bf16[16,256,128]{2,1,0:T(8,128)(2,1)} %get-tuple-element.21) | data formatting | bytes 2097152 | tf_op jit(solution)/shard_map/reshape | solution.py:40
  168.1 3.8 %reshape.307 = bf16[8192,64]{1,0:T(8,128)(2,1)} reshape(bf16[16,256,128]{2,1,0:T(8,128)(2,1)} %get-tuple-element.22) | data formatting | bytes 2097152 | tf_op jit(solution)/shard_map/reshape | solution.py:40
  171.9 2.6 fusion.34
  186.5 3.8 %copy.13 = f32[8192,64]{1,0:T(8,128)} copy(f32[8192,64]{0,1:T(8,128)} %fusion.1) | data formatting | bytes 4194304 | tf_op jit(solution)/shard_map/add | solution.py:46
  190.3 4.6 %reshape.337 = f32[16,256,128]{2,1,0:T(8,128)} reshape(f32[8192,64]{1,0:T(8,128)} %copy.13) | data formatting | bytes 4194304 | tf_op jit(solution)/shard_map/add | solution.py:46
  198.1 3.4 collective-permute-start.8
  204.7 3.8 %collective-permute-done.9 = bf16[1,256,128]{2,1,0:T(8,128)(2,1)S(1)} collective-permute-done((bf16[1,256,128]{2,1,0:T(8,128)(2,1)}, bf16[1,256,128]{2,1,0:T(8,128)(2,1)S(1)}, u32[]{:S(2)}, u32[]{:S(2)}) %collective-permute-start.9) | collective-permute-done | bytes 65568 | tf_op jit(solution)/shard_map/ppermute | solution.py:21
  209.9 3.8 %reshape.310 = bf16[8192,64]{1,0:T(8,128)(2,1)} reshape(bf16[16,256,128]{2,1,0:T(8,128)(2,1)} %get-tuple-element.43) | data formatting | bytes 2097152 | tf_op jit(solution)/shard_map/reshape | solution.py:40
  215.1 3.0 collective-permute-start.11
  218.1 3.8 %fusion.56 = f32[8192,64]{0,1:T(8,128)} fusion(bf16[8192,64]{1,0:T(8,128)(2,1)} %reshape.310, bf16[9,64,64]{2,1,0:T(8,128)(2,1)S(1)} %copy-done.30), kind=kOutput, calls=%fused_computation.117 | convolution fusion | flops 67108864 | bytes 3162112 | tf_op jit(solution)/shard_map/dot_general | solution.py:41
  222.0 4.0 %reshape.318 = bf16[8192,64]{1,0:T(8,128)(2,1)} reshape(bf16[16,256,128]{2,1,0:T(8,128)(2,1)} %get-tuple-element.42) | data formatting | bytes 2097152 | tf_op jit(solution)/shard_map/reshape | solution.py:40
  229.8 4.0 %reshape.309 = bf16[8192,64]{1,0:T(8,128)(2,1)} reshape(bf16[16,256,128]{2,1,0:T(8,128)(2,1)} %get-tuple-element.14) | data formatting | bytes 2097152 | tf_op jit(solution)/shard_map/reshape | solution.py:40
  235.7 3.9 %reshape.311 = bf16[8192,64]{1,0:T(8,128)(2,1)} reshape(bf16[16,256,128]{2,1,0:T(8,128)(2,1)} %get-tuple-element.17) | data formatting | bytes 2097152 | tf_op jit(solution)/shard_map/reshape | solution.py:40
  241.5 4.0 %reshape.314 = bf16[8192,64]{1,0:T(8,128)(2,1)} reshape(bf16[16,256,128]{2,1,0:T(8,128)(2,1)} %get-tuple-element.15) | data formatting | bytes 2097152 | tf_op jit(solution)/shard_map/reshape | solution.py:40
  247.3 3.8 %reshape.320 = bf16[8192,64]{1,0:T(8,128)(2,1)} reshape(bf16[16,256,128]{2,1,0:T(8,128)(2,1)} %get-tuple-element.16) | data formatting | bytes 2097152 | tf_op jit(solution)/shard_map/reshape | solution.py:40
  251.1 2.6 fusion.32
  265.7 3.8 %copy.14 = f32[8192,64]{1,0:T(8,128)} copy(f32[8192,64]{0,1:T(8,128)} %fusion) | data formatting | bytes 4194304 | tf_op jit(solution)/shard_map/add | solution.py:46
  269.6 4.7 %reshape.338 = f32[16,256,128]{2,1,0:T(8,128)} reshape(f32[8192,64]{1,0:T(8,128)} %copy.14) | data formatting | bytes 4194304 | tf_op jit(solution)/shard_map/add | solution.py:46
  274.3 5.0 %fusion.96 = (bf16[16,256,128]{2,1,0:T(8,128)(2,1)}, f32[16,256,128]{2,1,0:T(8,128)}) fusion(f32[16,256,128]{2,1,0:T(8,128)} %reshape.338, f32[16,256,128]{2,1,0:T(8,128)} %reshape.337, f32[16,256,128]{2,1,0:T(8,128)S(1)} %reshape.336, bf16[16,256,128]{2,1,0:T(8,128)(2,1)} %param.9, bf16[16,256,128]{2,1,0:T(8,128)(2,1)S(1)} %copy-done), kind=kLoop, calls=%fused_computation.167 | loop fusion | flops 6291456 | bytes 11534336 | tf_op jit(solution)/shard_map/convert_element_type | solution.py:70
  279.3 39.8 %scatter_custom_fusion.1 = bf16[8192,128]{1,0:T(8,128)(2,1)} fusion(s32[4096]{0:T(1024)} %bitcast.153, bf16[]{:T(256)} %constant.63.clone.1, pred[4096]{0:T(1024)(128)(4,1)S(1)} %compare_and_fusion, bf16[]{:T(256)} %constant.66.clone.1, bf16[4096,128]{1,0:T(8,128)(2,1)} %bitcast.142, s32[4096]{0:T(1024)S(1)} %fusion.67), kind=kCustom, calls=%fused_computation.66 | custom fusion | flops 524288 | bytes 3167232 | tf_op jit(solution)/shard_map/scatter | solution.py:86
  319.1 5.0 %all-to-all-start.1 = ((bf16[32,256,128]{2,1,0:T(8,128)(2,1)}), bf16[32,256,128]{2,1,0:T(8,128)(2,1)S(1)}, u32[]{:S(2)}, u32[]{:S(2)}) async-start(bf16[32,256,128]{2,1,0:T(8,128)(2,1)} %bitcast.21), calls=%async_computation.1 | async-start | bytes 4194304 | tf_op jit(solution)/shard_map/all_to_all | solution.py:89
  324.1 48.9 %all-to-all-done.1 = bf16[32,256,128]{2,1,0:T(8,128)(2,1)S(1)} async-done(((bf16[32,256,128]{2,1,0:T(8,128)(2,1)}), bf16[32,256,128]{2,1,0:T(8,128)(2,1)S(1)}, u32[]{:S(2)}, u32[]{:S(2)}) %all-to-all-start.1) | async-done | bytes 2097184 | tf_op jit(solution)/shard_map/all_to_all | solution.py:89
  374.2 3.3 convolution_bitcast_fusion.1
  (152 shorter events, 87.2 us)
Async XLA Ops:
  0.6 9.4 %copy-start.31 = (s32[4096,1]{0,1:T(1,128)S(1)}, s32[4096,1]{0,1:T(1,128)}, u32[]{:S(2)}) copy-start(s32[4096,1]{0,1:T(1,128)} %param.14) | copy-start | bytes 49156
  3.8 51.4 %collective-permute-start = (bf16[1,256,128]{2,1,0:T(8,128)(2,1)}, bf16[1,256,128]{2,1,0:T(8,128)(2,1)S(1)}, u32[]{:S(2)}, u32[]{:S(2)}) collective-permute-start(bf16[1,256,128]{2,1,0:T(8,128)(2,1)} %get-tuple-element.52), channel_id=1, source_target_pairs={{0,8},{8,16},{16,24},{1,9},{9,17},{17,25},{2,10},{10,18},{18,26},{... | collective-permute-start | bytes 196616 | tf_op jit(solution)/shard_map/ppermute | solution.py:20
  8.7 46.5 %collective-permute-start.1 = (bf16[1,256,128]{2,1,0:T(8,128)(2,1)S(1)}, bf16[1,256,128]{2,1,0:T(8,128)(2,1)S(1)}, u32[]{:S(2)}, u32[]{:S(2)}) collective-permute-start(bf16[1,256,128]{2,1,0:T(8,128)(2,1)S(1)} %get-tuple-element.53), channel_id=1, source_target_pairs={{8,0},{16,8},{24,16},{9,1},{17,9},{25,17},{10,2},{18,10},{26,18},{... | collective-permute-start | bytes 196616 | tf_op jit(solution)/shard_map/ppermute | solution.py:21
  31.1 24.1 %copy-start.33 = (s32[4096,1]{0,1:T(1,128)}, s32[4096,1]{0,1:T(1,128)S(1)}, u32[]{:S(2)}) copy-start(s32[4096,1]{0,1:T(1,128)S(1)} %compare_select_fusion) | copy-start | bytes 49156
  47.4 271.7 %all-to-all-start = ((s32[32,1,256]{2,1,0:T(1,128)}), s32[32,1,256]{2,1,0:T(1,128)S(1)}, u32[]{:S(2)}, u32[]{:S(2)}) async-start(s32[32,1,256]{2,1,0:T(1,128)} %bitcast.17), calls=%async_computation | async-start | bytes 65536 | tf_op jit(solution)/shard_map/all_to_all | solution.py:96
  55.2 17.5 %collective-permute-start.2 = (bf16[18,1,128]{2,1,0:T(2,128)(2,1)S(1)}, bf16[18,1,128]{2,1,0:T(2,128)(2,1)S(1)}, u32[]{:S(2)}, u32[]{:S(2)}) collective-permute-start(bf16[18,1,128]{2,1,0:T(2,128)(2,1)S(1)} %get-tuple-element.40), channel_id=1, source_target_pairs={{1,0},{2,1},{3,2},{4,3},{5,4},{6,5},{7,6},{9,8},{10,9},{11,10},{12... | collective-permute-start | bytes 13832 | tf_op jit(solution)/shard_map/ppermute | solution.py:21
  56.5 16.2 %collective-permute-start.3 = (bf16[18,1,128]{2,1,0:T(2,128)(2,1)S(1)}, bf16[18,1,128]{2,1,0:T(2,128)(2,1)S(1)}, u32[]{:S(2)}, u32[]{:S(2)}) collective-permute-start(bf16[18,1,128]{2,1,0:T(2,128)(2,1)S(1)} %get-tuple-element.41), channel_id=1, source_target_pairs={{0,1},{1,2},{2,3},{3,4},{4,5},{5,6},{6,7},{8,9},{9,10},{10,11},{11... | collective-permute-start | bytes 13832 | tf_op jit(solution)/shard_map/ppermute | solution.py:20
  61.2 3.9 %copy-start.30 = (bf16[9,64,64]{2,1,0:T(8,128)(2,1)S(1)}, bf16[9,64,64]{2,1,0:T(8,128)(2,1)}, u32[]{:S(2)}) copy-start(bf16[9,64,64]{2,1,0:T(8,128)(2,1)} %param.12) | copy-start | bytes 221188
  97.2 2.6 copy-start.7
  97.2 2.9 copy-start.21
  100.1 1.6 copy-start.22
  101.7 1.6 copy-start.18
  104.2 1.6 copy-start.15
  105.8 1.6 copy-start.10
  107.4 1.6 copy-start.25
  115.9 7.6 %copy-start.32 = (s32[4096]{0:T(1024)S(1)}, s32[4096]{0:T(1024)}, u32[]{:S(2)}) copy-start(s32[4096]{0:T(1024)} %param.13) | copy-start | bytes 49156
  118.5 6.8 %collective-permute-start.4 = (bf16[1,256,128]{2,1,0:T(8,128)(2,1)}, bf16[1,256,128]{2,1,0:T(8,128)(2,1)S(1)}, u32[]{:S(2)}, u32[]{:S(2)}) collective-permute-start(bf16[1,256,128]{2,1,0:T(8,128)(2,1)} %get-tuple-element.48), channel_id=1, source_target_pairs={{0,8},{8,16},{16,24},{1,9},{9,17},{17,25},{2,10},{10,18},{18,26},{... | collective-permute-start | bytes 196616 | tf_op jit(solution)/shard_map/ppermute | solution.py:20
  122.2 6.9 %collective-permute-start.5 = (bf16[1,256,128]{2,1,0:T(8,128)(2,1)}, bf16[1,256,128]{2,1,0:T(8,128)(2,1)S(1)}, u32[]{:S(2)}, u32[]{:S(2)}) collective-permute-start(bf16[1,256,128]{2,1,0:T(8,128)(2,1)} %get-tuple-element.49), channel_id=1, source_target_pairs={{8,0},{16,8},{24,16},{9,1},{17,9},{25,17},{10,2},{18,10},{26,18},{... | collective-permute-start | bytes 196616 | tf_op jit(solution)/shard_map/ppermute | solution.py:21
  134.4 12.4 %collective-permute-start.6 = (bf16[18,1,128]{2,1,0:T(2,128)(2,1)S(1)}, bf16[18,1,128]{2,1,0:T(2,128)(2,1)S(1)}, u32[]{:S(2)}, u32[]{:S(2)}) collective-permute-start(bf16[18,1,128]{2,1,0:T(2,128)(2,1)S(1)} %get-tuple-element.36), channel_id=1, source_target_pairs={{1,0},{2,1},{3,2},{4,3},{5,4},{6,5},{7,6},{9,8},{10,9},{11,10},{12... | collective-permute-start | bytes 13832 | tf_op jit(solution)/shard_map/ppermute | solution.py:21
  135.7 11.1 %collective-permute-start.7 = (bf16[18,1,128]{2,1,0:T(2,128)(2,1)S(1)}, bf16[18,1,128]{2,1,0:T(2,128)(2,1)S(1)}, u32[]{:S(2)}, u32[]{:S(2)}) collective-permute-start(bf16[18,1,128]{2,1,0:T(2,128)(2,1)S(1)} %get-tuple-element.37), channel_id=1, source_target_pairs={{0,1},{1,2},{2,3},{3,4},{4,5},{5,6},{6,7},{8,9},{9,10},{10,11},{11... | collective-permute-start | bytes 13832 | tf_op jit(solution)/shard_map/ppermute | solution.py:20
  150.6 4.0 %copy-start.1 = (bf16[18,257,128]{2,1,0:T(8,128)(2,1)S(1)}, bf16[18,257,128]{2,1,0:T(8,128)(2,1)}, u32[]{:S(2)}) copy-start(bf16[18,257,128]{2,1,0:T(8,128)(2,1)} %get-tuple-element.35) | copy-start | bytes 3552772
  156.5 3.9 %copy-start.28 = (bf16[16,256,128]{2,1,0:T(8,128)(2,1)S(1)}, bf16[16,256,128]{2,1,0:T(8,128)(2,1)}, u32[]{:S(2)}) copy-start(bf16[16,256,128]{2,1,0:T(8,128)(2,1)} %get-tuple-element.19) | copy-start | bytes 3145732
  162.2 4.0 %copy-start.26 = (bf16[16,256,128]{2,1,0:T(8,128)(2,1)S(1)}, bf16[16,256,128]{2,1,0:T(8,128)(2,1)}, u32[]{:S(2)}) copy-start(bf16[16,256,128]{2,1,0:T(8,128)(2,1)} %get-tuple-element.18) | copy-start | bytes 3145732
  171.9 2.6 copy-start.5
  171.9 2.9 copy-start.8
  174.7 1.6 copy-start.19
  176.3 1.6 copy-start.16
  177.9 1.6 copy-start.3
  179.5 1.6 copy-start.11
  181.1 1.6 copy-start.12
  182.7 1.6 copy-start.23
  198.1 6.5 %collective-permute-start.8 = (bf16[1,256,128]{2,1,0:T(8,128)(2,1)}, bf16[1,256,128]{2,1,0:T(8,128)(2,1)S(1)}, u32[]{:S(2)}, u32[]{:S(2)}) collective-permute-start(bf16[1,256,128]{2,1,0:T(8,128)(2,1)} %get-tuple-element.44), channel_id=1, source_target_pairs={{0,8},{8,16},{16,24},{1,9},{9,17},{17,25},{2,10},{10,18},{18,26},{... | collective-permute-start | bytes 196616 | tf_op jit(solution)/shard_map/ppermute | solution.py:20
  201.5 7.0 %collective-permute-start.9 = (bf16[1,256,128]{2,1,0:T(8,128)(2,1)}, bf16[1,256,128]{2,1,0:T(8,128)(2,1)S(1)}, u32[]{:S(2)}, u32[]{:S(2)}) collective-permute-start(bf16[1,256,128]{2,1,0:T(8,128)(2,1)} %get-tuple-element.45), channel_id=1, source_target_pairs={{8,0},{16,8},{24,16},{9,1},{17,9},{25,17},{10,2},{18,10},{26,18},{... | collective-permute-start | bytes 196616 | tf_op jit(solution)/shard_map/ppermute | solution.py:21
  213.8 12.2 %collective-permute-start.10 = (bf16[18,1,128]{2,1,0:T(2,128)(2,1)S(1)}, bf16[18,1,128]{2,1,0:T(2,128)(2,1)S(1)}, u32[]{:S(2)}, u32[]{:S(2)}) collective-permute-start(bf16[18,1,128]{2,1,0:T(2,128)(2,1)S(1)} %get-tuple-element.32), channel_id=1, source_target_pairs={{1,0},{2,1},{3,2},{4,3},{5,4},{6,5},{7,6},{9,8},{10,9},{11,10},{12... | collective-permute-start | bytes 13832 | tf_op jit(solution)/shard_map/ppermute | solution.py:21
  215.1 10.9 %collective-permute-start.11 = (bf16[18,1,128]{2,1,0:T(2,128)(2,1)S(1)}, bf16[18,1,128]{2,1,0:T(2,128)(2,1)S(1)}, u32[]{:S(2)}, u32[]{:S(2)}) collective-permute-start(bf16[18,1,128]{2,1,0:T(2,128)(2,1)S(1)} %get-tuple-element.33), channel_id=1, source_target_pairs={{0,1},{1,2},{2,3},{3,4},{4,5},{5,6},{6,7},{8,9},{9,10},{10,11},{11... | collective-permute-start | bytes 13832 | tf_op jit(solution)/shard_map/ppermute | solution.py:20
  229.8 4.0 %copy-start.2 = (bf16[18,257,128]{2,1,0:T(8,128)(2,1)S(1)}, bf16[18,257,128]{2,1,0:T(8,128)(2,1)}, u32[]{:S(2)}) copy-start(bf16[18,257,128]{2,1,0:T(8,128)(2,1)} %get-tuple-element.31) | copy-start | bytes 3552772
  235.7 3.9 %copy-start.29 = (bf16[16,256,128]{2,1,0:T(8,128)(2,1)S(1)}, bf16[16,256,128]{2,1,0:T(8,128)(2,1)}, u32[]{:S(2)}) copy-start(bf16[16,256,128]{2,1,0:T(8,128)(2,1)} %get-tuple-element.13) | copy-start | bytes 3145732
  241.5 4.0 %copy-start.27 = (bf16[16,256,128]{2,1,0:T(8,128)(2,1)S(1)}, bf16[16,256,128]{2,1,0:T(8,128)(2,1)}, u32[]{:S(2)}) copy-start(bf16[16,256,128]{2,1,0:T(8,128)(2,1)} %get-tuple-element.12) | copy-start | bytes 3145732
  251.1 2.6 copy-start.6
  251.1 2.9 copy-start.9
  254.0 1.6 copy-start.20
  255.5 1.6 copy-start.17
  257.1 1.6 copy-start.4
  258.7 1.6 copy-start.13
  260.3 1.6 copy-start.14
  269.6 4.7 %copy-start = (bf16[16,256,128]{2,1,0:T(8,128)(2,1)S(1)}, bf16[16,256,128]{2,1,0:T(8,128)(2,1)}, u32[]{:S(2)}) copy-start(bf16[16,256,128]{2,1,0:T(8,128)(2,1)} %param.10) | copy-start | bytes 3145732
  319.1 53.9 %all-to-all-start.1 = ((bf16[32,256,128]{2,1,0:T(8,128)(2,1)}), bf16[32,256,128]{2,1,0:T(8,128)(2,1)S(1)}, u32[]{:S(2)}, u32[]{:S(2)}) async-start(bf16[32,256,128]{2,1,0:T(8,128)(2,1)} %bitcast.21), calls=%async_computation.1 | async-start | bytes 4194304 | tf_op jit(solution)/shard_map/all_to_all | solution.py:89
  374.2 3.3 copy-start.35
  (2 other events, 2.6 us)
where the time goes:
time: 387 us; the launch traced here: 381 us
  local copies, waits for them, and re-layouts  156 us (40%)
  other arithmetic  80.4 us (21%)
  waiting for transfers between devices  56.5 us (15%)
  matrix products  45.6 us (12%)
  starting transfers between devices  40.9 us (11%)
    reshape x27, local copies, waits for them, and re-layouts, stiffness_apply(): flattened = source.reshape(-1, stiffness.shape[1])  88 us
    all_to_all x1, waiting for transfers between devices, local(): lax.all_to_all(buffer.reshape(devices, slot_total, row_width), ('gx', 'gy...  48.9 us
    dot_general x27, matrix products, stiffness_apply(): jnp.dot(flattened, stiffness[3 * (shift_row + 1) + (shift_col + 1)], pref...  40.5 us
    scatter x1, other arithmetic, local(): jnp.zeros((devices * slot_total, row_width), jnp.bfloat16).at[targets]  39.8 us
    add x6, local copies, waits for them, and re-layouts, stiffness_apply(): summed = summed + product.reshape(out_rows, out_cols, -1)  23 us
    ppermute x6, starting transfers between devices, extended(): before = lax.ppermute(last, axis, up)  21.2 us
    another operation x3, other arithmetic  19 us
    scatter x1, local copies, waits for them, and re-layouts, local(): jnp.full((devices * slot_total,), -1, jnp.int32).at[targets].set(row_pos)  16.3 us
  transfers between devices with their start and end apart: 14, of which 3 were waited for; matrix products, arithmetic and copies ran while one was open for 68% of the time, Pallas kernels for 0%

commit v1 on v0

v1 whole, which is shorter than its diff:
```python
import functools

import jax
import jax.numpy as jnp
from jax import lax
from jax.experimental import pallas as pl
from jax.experimental.pallas import tpu as pltpu
from jax.sharding import PartitionSpec as P

LEVELS = 16

soft_floor = 0.001
relax_rate = 0.5

MESH = pl.DeviceIdType.MESH
PASSES = 3
SIDES = ((-1, 0), (1, 0), (0, -1), (0, 1), (-1, -1), (-1, 1), (1, -1), (1, 1))


def cell_weight(levels):
    ratio = levels.astype(jnp.float32) / LEVELS
    return soft_floor + (1.0 - soft_floor) * ratio * ratio * ratio


def relax_kernel(
    size_x,
    size_y,
    grad_ref,
    start_ref,
    weight_ref,
    blocks_ref,
    lam_ref,
    wide_ref,
    shifted_ref,
    line_ref,
    big_ref,
    edge_ref,
    edge_send_ref,
    row_in_ref,
    col_in_ref,
    send_sem,
    recv_sem,
):
    rows, cols, width = grad_ref.shape
    gx, gy = lax.axis_index("gx"), lax.axis_index("gy")

    def exists(side):
        dx, dy = side
        held = None
        for here, step, size in ((gx, dx, size_x), (gy, dy, size_y)):
            if step:
                inside = (here + step >= 0) & (here + step < size)
                held = inside if held is None else held & inside
        return held

    def place(side):
        return (gx + side[0], gy + side[1])

    row_in_ref[...] = jnp.zeros_like(row_in_ref)
    col_in_ref[...] = jnp.zeros_like(col_in_ref)

    barrier = pltpu.get_barrier_semaphore()
    for side in SIDES:

        @pl.when(exists(side))
        def _(side=side):
            pl.semaphore_signal(barrier, inc=1, device_id=place(side), device_id_type=MESH)

    for b in range(3):
        shifted_ref[b, 0] = jnp.zeros((cols, width), jnp.bfloat16)
        shifted_ref[b, rows + 1] = jnp.zeros((cols, width), jnp.bfloat16)
    line_ref[0:8, :] = jnp.zeros((8, width), jnp.float32)
    line_ref[8 + cols : 16 + cols, :] = jnp.zeros((8, width), jnp.float32)

    for i in range(4):
        for b in range(3):
            for j in range(2):
                a = j + 1 - i
                at = (pl.ds((3 * i + b) * width, width), pl.ds(j * width, width))
                if -1 <= a <= 1:
                    big_ref[at] = blocks_ref[3 * (a + 1) + b]
                else:
                    big_ref[at] = jnp.zeros((width, width), jnp.bfloat16)

    for r in range(rows):
        wide_ref[r] = jnp.broadcast_to(weight_ref[:, r : r + 1], (cols, width))

    def take_start(r, carry):
        lam_ref[r] = start_ref[r].astype(jnp.float32)
        return carry

    lax.fori_loop(0, rows, take_start, 0)

    near_x = 1 + jnp.minimum(gx, 1) + jnp.minimum(size_x - 1 - gx, 1)
    near_y = 1 + jnp.minimum(gy, 1) + jnp.minimum(size_y - 1 - gy, 1)
    pl.semaphore_wait(barrier, near_x * near_y - 1)

    def copies(step):
        made = []
        for n, side in enumerate(SIDES):
            if side[1] == 0:
                source = shifted_ref.at[1, 1 if side[0] < 0 else rows]
                target = row_in_ref.at[step, 1 if side[0] < 0 else 0]
            else:
                source = edge_send_ref.at[0 if side[1] < 0 else 1]
                target = col_in_ref.at[step, SIDES.index((-side[0], -side[1])) - 2]
            made.append(
                pltpu.make_async_remote_copy(
                    src_ref=source,
                    dst_ref=target,
                    send_sem=send_sem.at[step, n],
                    recv_sem=recv_sem.at[step, SIDES.index((-side[0], -side[1]))],
                    device_id=place(side),
                    device_id_type=MESH,
                )
            )
        return made

    def arrivals(step):
        made = []
        for n, side in enumerate(SIDES):
            if side[1] == 0:
                target = row_in_ref.at[step, 0 if side[0] < 0 else 1]
            else:
                target = col_in_ref.at[step, n - 2]
            made.append((side, target, recv_sem.at[step, n]))
        return made

    def spread():
        return [line_ref[9 - b : 9 - b + cols, :].astype(jnp.bfloat16) for b in range(3)]

    for step in range(PASSES):

        def produce(r, carry):
            scaled = wide_ref[r] * lam_ref[r]
            line_ref[8 : 8 + cols, :] = scaled
            left, middle, right = spread()
            shifted_ref[0, r + 1] = left
            shifted_ref[1, r + 1] = middle
            shifted_ref[2, r + 1] = right
            edge_ref[0, pl.ds(r, 1), :] = scaled[0:1, :]
            edge_ref[1, pl.ds(r, 1), :] = scaled[cols - 1 : cols, :]
            return carry

        lax.fori_loop(0, rows, produce, 0)
        edge_send_ref[...] = edge_ref[:, 0:rows, :].astype(jnp.bfloat16)

        sends = copies(step)
        for side, copy in zip(SIDES, sends):

            @pl.when(exists(side))
            def _(copy=copy):
                copy.start()

        def interior(t, carry):
            r = 4 * t
            lhs = jnp.concatenate(
                [
                    jnp.concatenate(
                        [shifted_ref[b, r + 2 * p + i] for i in range(4) for b in range(3)], axis=1
                    )
                    for p in range(2)
                ],
                axis=0,
            )
            image = jnp.dot(lhs, big_ref[...], preferred_element_type=jnp.float32)
            for p in range(2):
                for j in range(2):
                    at = r + 2 * p + j
                    part = image[p * cols : (p + 1) * cols, j * width : (j + 1) * width]
                    lam_ref[at] = lam_ref[at] + relax_rate * (
                        grad_ref[at].astype(jnp.float32) - part
                    )
            return carry

        lax.fori_loop(0, rows // 4, interior, 0)

        for n, (side, copy) in enumerate(zip(SIDES, sends)):

            @pl.when(exists(side))
            def _(copy=copy):
                copy.wait_send()

        for side, copy in zip(SIDES, sends):

            @pl.when(exists(side))
            def _(side=side, step=step):
                target, semaphore = [x[1:] for x in arrivals(step) if x[0] == side][0]
                pltpu.make_async_remote_copy(
                    src_ref=target,
                    dst_ref=target,
                    send_sem=send_sem.at[step, 0],
                    recv_sem=semaphore,
                    device_id=place(side),
                    device_id_type=MESH,
                ).wait_recv()

        for end in range(2):
            line_ref[8 : 8 + cols, :] = row_in_ref[step, end].astype(jnp.float32)
            lhs = jnp.concatenate(spread(), axis=1)
            depth = 3 * width
            piece = (
                big_ref[0:depth, 0:width]
                if end == 0
                else big_ref[3 * depth : 4 * depth, width : 2 * width]
            )
            more = jnp.dot(lhs, piece, preferred_element_type=jnp.float32)
            at = 0 if end == 0 else rows - 1
            lam_ref[at] = lam_ref[at] - relax_rate * more

        for end in range(2):
            edge_ref[end, 8 : 8 + rows, :] = col_in_ref[step, end].astype(jnp.float32)
            upper = col_in_ref[step, 2 + end].astype(jnp.float32)
            lower = col_in_ref[step, 4 + end].astype(jnp.float32)
            edge_ref[end, 7:8, :] = upper[rows - 1 : rows, :]
            edge_ref[end, 8 + rows : 9 + rows, :] = lower[0:1, :]
            b = 2 if end == 0 else 0
            more = jnp.zeros((rows, width), jnp.float32)
            for a in (-1, 0, 1):
                source = edge_ref[end, 8 - a : 8 - a + rows, :].astype(jnp.bfloat16)
                more = more + jnp.dot(
                    source, blocks_ref[3 * (a + 1) + b], preferred_element_type=jnp.float32
                )
            at = 0 if end == 0 else cols - 1
            for r in range(rows):
                lam_ref[r, at : at + 1, :] = (
                    lam_ref[r, at : at + 1, :] - relax_rate * more[r : r + 1, :]
                )


def relax(grad, start, weight, blocks, size_x, size_y):
    rows, cols, width = grad.shape
    vmem = pl.BlockSpec(memory_space=pltpu.VMEM)
    return pl.pallas_call(
        functools.partial(relax_kernel, size_x, size_y),
        out_shape=jax.ShapeDtypeStruct((rows, cols, width), jnp.float32),
        in_specs=[vmem] * 4,
        out_specs=vmem,
        scratch_shapes=[
            pltpu.VMEM((rows, cols, width), jnp.float32),
            pltpu.VMEM((3, rows + 2, cols, width), jnp.bfloat16),
            pltpu.VMEM((cols + 16, width), jnp.float32),
            pltpu.VMEM((12 * width, 2 * width), jnp.bfloat16),
            pltpu.VMEM((2, rows + 16, width), jnp.float32),
            pltpu.VMEM((2, rows, width), jnp.bfloat16),
            pltpu.VMEM((PASSES, 2, cols, width), jnp.bfloat16),
            pltpu.VMEM((PASSES, 6, rows, width), jnp.bfloat16),
            pltpu.SemaphoreType.DMA((PASSES, 8)),
            pltpu.SemaphoreType.DMA((PASSES, 8)),
        ],
        compiler_params=pltpu.CompilerParams(
            collective_id=0, has_side_effects=True, vmem_limit_bytes=48 * 1024 * 1024
        ),
        cost_estimate=pl.CostEstimate(
            flops=6 * 2 * rows * cols * width * 9 * width,
            bytes_accessed=8 * rows * cols * width,
            transcendentals=0,
        ),
    )(grad, start, weight, blocks)


def table_kernel(front_ref, cell_ref, pos_ref, place_ref, cells_ref, spots_ref, sums_ref):
    count, capacity = cells_ref.shape
    total = front_ref.shape[1]
    block = 256
    order = lax.broadcasted_iota(jnp.int32, (count, count), 0)
    moved = (order == place_ref[...]).astype(jnp.float32).astype(jnp.bfloat16)
    before = (
        lax.broadcasted_iota(jnp.int32, (block, block), 0)
        < lax.broadcasted_iota(jnp.int32, (block, block), 1)
    )
    before = before.astype(jnp.float32).astype(jnp.bfloat16)
    carry = jnp.zeros((count, 1), jnp.float32)
    sums_ref[...] = jnp.zeros_like(sums_ref)
    for n in range(total // block):
        at = slice(n * block, (n + 1) * block)
        named = lax.broadcasted_iota(jnp.int32, (count, block), 0) == front_ref[:, at]
        named = named.astype(jnp.float32).astype(jnp.bfloat16)
        member = jnp.dot(moved, named, preferred_element_type=jnp.float32)
        inside = jnp.dot(
            member.astype(jnp.bfloat16), before, preferred_element_type=jnp.float32
        )
        rank = jnp.sum(member * (inside + carry), axis=0, keepdims=True)
        carry = carry + jnp.sum(member, axis=1, keepdims=True)
        slot = lax.broadcasted_iota(jnp.int32, (capacity, block), 0) == rank.astype(jnp.int32)
        slot = slot.astype(jnp.float32).astype(jnp.bfloat16)
        cell, pos = cell_ref[:, at], pos_ref[:, at]
        pieces = (cell // 64, cell % 64, pos // 16, pos % 16 + 1)
        lhs = jnp.concatenate([member * p.astype(jnp.float32) for p in pieces], axis=0)
        sums_ref[...] += lax.dot_general(
            lhs.astype(jnp.bfloat16),
            slot,
            (((1,), (1,)), ((), ())),
            preferred_element_type=jnp.float32,
        )
    part = [sums_ref[n * count : (n + 1) * count, :].astype(jnp.int32) for n in range(4)]
    cells_ref[...] = part[0] * 64 + part[1]
    spots_ref[...] = part[2] * 16 + part[3] - 1


def row_table(row_front, row_cells, row_pos, front_place, capacity):
    count = front_place.shape[0]
    shape = jax.ShapeDtypeStruct((count, capacity), jnp.int32)
    return pl.pallas_call(
        table_kernel,
        out_shape=(shape, shape),
        in_specs=[pl.BlockSpec(memory_space=pltpu.VMEM)] * 4,
        out_specs=(pl.BlockSpec(memory_space=pltpu.VMEM),) * 2,
        scratch_shapes=[pltpu.VMEM((4 * count, capacity), jnp.float32)],
        compiler_params=pltpu.CompilerParams(vmem_limit_bytes=32 * 1024 * 1024),
    )(
        row_front.reshape(1, -1),
        row_cells.reshape(1, -1),
        row_pos.reshape(1, -1),
        front_place.reshape(1, -1),
    )


def pick_kernel(cells_ref, field_ref, out_ref, held_ref):
    total = out_ref.shape[0]
    step = 32

    def some(t, carry):
        for u in range(step):
            at = t * step + u
            held_ref[pl.ds(at, 1), :] = field_ref[pl.ds(cells_ref[at], 1), :]
        return carry

    lax.fori_loop(0, total // step, some, 0)
    out_ref[...] = held_ref[...].astype(out_ref.dtype)


def pick(cells, field):
    total, width = cells.shape[0], field.shape[1]
    vmem = pl.BlockSpec(memory_space=pltpu.VMEM)
    return pl.pallas_call(
        pick_kernel,
        out_shape=jax.ShapeDtypeStruct((total, width), jnp.bfloat16),
        in_specs=[pl.BlockSpec(memory_space=pltpu.SMEM), vmem],
        out_specs=vmem,
        scratch_shapes=[pltpu.VMEM((total, width), jnp.float32)],
        compiler_params=pltpu.CompilerParams(vmem_limit_bytes=32 * 1024 * 1024),
    )(cells, field)


def local(
    size_x,
    size_y,
    objective_grad,
    adjoint_start,
    levels,
    stiffness,
    row_cells,
    row_front,
    row_pos,
    front_place,
    schur,
):
    rows, cols, width = objective_grad.shape
    freedom = stiffness.shape[1]
    cases = width // freedom
    same = jnp.eye(cases, dtype=stiffness.dtype)
    blocks = (same[None, :, None, :, None] * stiffness[:, None, :, None, :]).reshape(
        9, width, width
    )
    adjoint = relax(
        objective_grad, adjoint_start, cell_weight(levels).T, blocks, size_x, size_y
    )

    front_count = front_place.shape[0]
    devices = size_x * size_y
    owned, front_size = schur.shape[0], schur.shape[1]
    capacity = 2 * row_cells.shape[0] // front_count
    cells, spots = row_table(row_front, row_cells, row_pos, front_place, capacity)
    rows_out = pick(cells.reshape(-1), adjoint.reshape(rows * cols, width))
    slot_total = owned * capacity
    spread = functools.partial(
        lax.all_to_all, axis_name=("gx", "gy"), split_axis=0, concat_axis=0, tiled=True
    )
    spots_in = spread(spots.reshape(devices, slot_total)).reshape(devices, owned, capacity)
    rows_in = spread(rows_out.reshape(devices, slot_total, width))
    rows_in = rows_in.reshape(devices, owned, capacity, width)
    results = []
    for slot in range(owned):
        slot_rows = rows_in[:, slot].reshape(devices * capacity, width)
        slot_spots = spots_in[:, slot].reshape(devices * capacity)
        selector = (
            jnp.arange(front_size, dtype=jnp.int32)[:, None] == slot_spots[None, :]
        ).astype(jnp.bfloat16)
        assembled = jnp.dot(selector, slot_rows, preferred_element_type=jnp.float32)
        assembled = assembled.astype(jnp.bfloat16)
        results.append(jnp.dot(schur[slot], assembled, preferred_element_type=jnp.float32))
    return (adjoint, jnp.stack(results))


def solution(mesh):
    placed = (
        P("gx", "gy", None),
        P("gx", "gy", None),
        P("gx", "gy"),
        P(),
        P(("gx", "gy")),
        P(("gx", "gy"), None),
        P(("gx", "gy")),
        P(),
        P(("gx", "gy"), None, None),
    )
    return jax.shard_map(
        functools.partial(local, mesh.shape["gx"], mesh.shape["gy"]),
        mesh=mesh,
        in_specs=placed,
        out_specs=(P("gx", "gy", None), P(("gx", "gy"), None, None)),
        check_vma=False,
    )
```

time: 387 us -> 114 us (0.29); the launches traced: 381 us -> 113 us
  local copies, waits for them, and re-layouts: 156 us -> 12.5 us
  other arithmetic: 80.4 us -> 2.48 us
  matrix products: 45.6 us -> 6.74 us
  Pallas kernels: 0 us -> 30 us
  starting transfers between devices: 40.9 us -> 11.9 us
  waiting for transfers between devices: 56.5 us -> 48.8 us
    reshape x27 -> x0, local copies, waits for them, and re-layouts: 88 us -> none  [stiffness_apply(): flattened = source.reshape(-1, stiffness.shape[1])]
    dot_general x27 -> x0, matrix products: 40.5 us -> none  [stiffness_apply(): jnp.dot(flattened, stiffness[3 * (shift_row + 1) + (shift_col + 1)], pref...]
    scatter x1 -> x0, other arithmetic: 39.8 us -> none  [local(): jnp.zeros((devices * slot_total, row_width), jnp.bfloat16).at[targets]]
    pallas_call x0 -> x3, Pallas kernels: none -> 30 us  [the longest x1 17.6 us: relax(): pl.pallas_call(functools.partial(relax_kernel, size_x, size_y), out_shape...]
    ppermute x12 -> x0, starting transfers between devices: 29 us -> none  [the longest x6 21.2 us: extended(): before = lax.ppermute(last, axis, up)]
    add x6 -> x0, local copies, waits for them, and re-layouts: 23 us -> none  [stiffness_apply(): summed = summed + product.reshape(out_rows, out_cols, -1)]
    another operation x4 -> x1, other arithmetic: 19 us -> 0.98 us  [local(): return (adjoint, jnp.stack(results))]
    scatter x1 -> x0, local copies, waits for them, and re-layouts: 16.3 us -> none  [local(): jnp.full((devices * slot_total,), -1, jnp.int32).at[targets].set(row_pos)]
  transfers between devices with their start and end apart: 14 -> 2, of which waited for: 3 -> 1; matrix products, arithmetic and copies ran while one was open for 68% -> 3% of each run, Pallas kernels for 0% -> 23%
where the time goes in v1:
time: 114 us; the launch traced here: 113 us
  waiting for transfers between devices  48.8 us (43%)
  Pallas kernels  30 us (26%)
  local copies, waits for them, and re-layouts  12.5 us (11%)
  starting transfers between devices  11.9 us (10%)
  matrix products  6.74 us (6%)
  other arithmetic  2.48 us (2%)
    all_to_all x1, waiting for transfers between devices, local(): rows_in = spread(rows_out.reshape(devices, slot_total, width))  48.8 us
    pallas_call x1, Pallas kernels, relax(): pl.pallas_call(functools.partial(relax_kernel, size_x, size_y), out_shape...  17.6 us
    pallas_call x1, Pallas kernels, pick(): pl.pallas_call(pick_kernel, out_shape=jax.ShapeDtypeStruct((total, width)...  8.82 us
    unnamed x16, local copies, waits for them, and re-layouts  7.65 us
    all_to_all x1, starting transfers between devices, local(): spread(spots.reshape(devices, slot_total)).reshape(devices, owned, capacity)  7.3 us
    dot_general x2, matrix products, local(): jnp.dot(schur[slot], assembled, preferred_element_type=jnp.float32)  6.74 us
    all_to_all x1, starting transfers between devices, local(): rows_in = spread(rows_out.reshape(devices, slot_total, width))  4.59 us
    pallas_call x1, Pallas kernels, row_table(): pl.pallas_call(table_kernel, out_shape=(shape, shape), in_specs=[pl.Block...  3.59 us
  transfers between devices with their start and end apart: 2, of which 1 were waited for; matrix products, arithmetic and copies ran while one was open for 3% of the time, Pallas kernels for 23%

profile of v1, /device:TPU:0, one launch (start us, length us, event | category | flops | bytes accessed | tf_op | source)
XLA Modules:
  0.0 113.2 jit_solution(10014859071549319056)
XLA Ops:
  0.6 0.0 copy-start.1
  0.6 0.7 copy-done.1
  1.3 0.0 copy-start.2
  1.4 0.7 copy-done.2
  2.1 0.0 copy-start.3
  2.1 0.7 copy-done.3
  2.8 0.0 copy-start.4
  2.8 0.7 copy-done.4
  3.4 0.0 copy-start.5
  3.4 3.6 %shard_map.105 = (s32[64,128]{1,0:T(8,128)S(1)}, s32[64,128]{1,0:T(8,128)}) custom-call(s32[1,4096]{1,0:T(1,128)S(1)} %bitcast.35, s32[1,4096]{1,0:T(1,128)S(1)} %bitcast.36, s32[1,4096]{1,0:T(1,128)S(1)} %bitcast.37, s32[1,64]{1,0:T(1,128)S(1)} %bitcast.38), custom_call_target="tpu_custom_call" | custom-call | tf_op jit(solution)/shard_map/pallas_call | solution.py:304
  7.0 7.3 %all-to-all-start = ((s32[32,1,256]{2,1,0:T(1,128)}), s32[32,1,256]{2,1,0:T(1,128)S(1)}, u32[]{:S(2)}, u32[]{:S(2)}) async-start(s32[32,1,256]{2,1,0:T(1,128)} %bitcast.5), calls=%async_computation | async-start | bytes 65536 | tf_op jit(solution)/shard_map/all_to_all | solution.py:380
  14.4 0.7 broadcast_multiply_fusion.1
  15.1 0.7 convert_element_type.18
  15.8 0.1 mul.36
  15.9 0.1 mul.37
  16.0 0.1 copy.17
  16.1 0.1 copy.18
  16.2 1.3 %mul.39 = bf16[9,2,64,2,64]{4,3,2,1,0:T(2,128)(2,1)S(1)} broadcast(bf16[9,64,64]{2,1,0:T(8,128)(2,1)} %param.12), dimensions={0,2,4} | broadcast | bytes 368640 | tf_op jit(solution)/shard_map/mul | solution.py:363
  17.6 0.3 mul.40
  17.9 0.0 copy-done.5
  17.9 0.0 copy-start.6
  17.9 1.2 %copy-done.6 = bf16[16,256,128]{2,1,0:T(8,128)(2,1)S(1)} copy-done((bf16[16,256,128]{2,1,0:T(8,128)(2,1)S(1)}, bf16[16,256,128]{2,1,0:T(8,128)(2,1)}, u32[]{:S(2)}) %copy-start.6) | copy-done | bytes 1048600
  19.1 17.6 %shard_map.104 = f32[16,256,128]{2,1,0:T(8,128)S(1)} custom-call(bf16[16,256,128]{2,1,0:T(8,128)(2,1)S(1)} %copy-done.5, bf16[16,256,128]{2,1,0:T(8,128)(2,1)S(1)} %copy-done.6, f32[256,16]{1,0:T(8,128)S(1)} %fusion.11.weight_ref, bf16[9,128,128]{2,1,0:T(8,128)(2,1)S(1)} %broadcast_multiply_fusion.blocks_ref), custom_call_target="tpu_custom_call" | custom-call | flops 7247757312 | bytes 4194304 | tf_op jit(solution)/shard_map/pallas_call | solution.py:234
  36.7 8.8 %shard_map.106 = bf16[8192,128]{1,0:T(8,128)(2,1)S(1)} custom-call(s32[8192]{0:T(1024)S(1)} %bitcast.34, f32[4096,128]{1,0:T(8,128)S(1)} %bitcast.32), custom_call_target="tpu_custom_call" | custom-call | tf_op jit(solution)/shard_map/pallas_call | solution.py:336
  45.6 0.0 copy-start
  45.6 1.3 %copy-done = bf16[8192,128]{1,0:T(8,128)(2,1)} copy-done((bf16[8192,128]{1,0:T(8,128)(2,1)}, bf16[8192,128]{1,0:T(8,128)(2,1)S(1)}, u32[]{:S(2)}) %copy-start) | copy-done | bytes 2097176
  46.9 0.0 all-to-all-done
  46.9 4.6 %all-to-all-start.1 = ((bf16[32,256,128]{2,1,0:T(8,128)(2,1)}), bf16[32,256,128]{2,1,0:T(8,128)(2,1)}, u32[]{:S(2)}, u32[]{:S(2)}) async-start(bf16[32,256,128]{2,1,0:T(8,128)(2,1)} %bitcast.33), calls=%async_computation.1 | async-start | bytes 4194304 | tf_op jit(solution)/shard_map/all_to_all | solution.py:381
  51.5 48.8 %all-to-all-done.1 = bf16[32,256,128]{2,1,0:T(8,128)(2,1)} async-done(((bf16[32,256,128]{2,1,0:T(8,128)(2,1)}), bf16[32,256,128]{2,1,0:T(8,128)(2,1)}, u32[]{:S(2)}, u32[]{:S(2)}) %all-to-all-start.1) | async-done | bytes 2097184 | tf_op jit(solution)/shard_map/all_to_all | solution.py:381
  100.3 2.8 %fusion.12 = (bf16[32,1,128,128]{3,2,1,0:T(8,128)(2,1)}, bf16[32,1,128,128]{3,2,1,0:T(8,128)(2,1)S(1)}) fusion(bf16[32,2,128,128]{3,2,1,0:T(8,128)(2,1)} %bitcast.11), kind=kLoop, calls=%fused_computation.21 | loop fusion | bytes 4194304 | tf_op jit(solution)/shard_map/slice | solution.py:385
  103.1 3.2 %convolution_bitcast_fusion.1 = f32[1,512,128]{1,2,0:T(8,128)S(1)} fusion(bf16[4096,128]{1,0:T(8,128)(2,1)} %bitcast.40, s32[4096]{0:T(1024)S(1)} %bitcast.43, bf16[2,512,512]{2,1,0:T(8,128)(2,1)} %param.17), kind=kOutput, calls=%fused_computation.7 | convolution fusion | flops 606142464 | bytes 1851392 | tf_op jit(solution)/shard_map/dot_general | solution.py:392
  106.3 3.6 %convolution_bitcast_fusion = f32[1,512,128]{1,2,0:T(8,128)} fusion(bf16[4096,128]{1,0:T(8,128)(2,1)S(1)} %bitcast.39, s32[4096]{0:T(1024)S(1)} %bitcast.42, bf16[2,512,512]{2,1,0:T(8,128)(2,1)} %param.17), kind=kOutput, calls=%fused_computation.6 | convolution fusion | flops 606142464 | bytes 1851392 | tf_op jit(solution)/shard_map/dot_general | solution.py:392
  109.9 1.0 pad_maximum_fusion
  110.8 1.0 copy.20
  111.8 1.3 %copy.22 = f32[16,256,128]{2,1,0:T(8,128)} copy(f32[16,256,128]{2,1,0:T(8,128)S(1)} %shard_map.104) | data formatting | bytes 4194304
  (4 shorter events, 0.1 us)
Async XLA Ops:
  0.6 0.7 copy-start.1
  1.3 0.7 copy-start.2
  2.1 0.7 copy-start.3
  2.8 0.7 copy-start.4
  3.4 14.5 %copy-start.5 = (bf16[16,256,128]{2,1,0:T(8,128)(2,1)S(1)}, bf16[16,256,128]{2,1,0:T(8,128)(2,1)}, u32[]{:S(2)}) copy-start(bf16[16,256,128]{2,1,0:T(8,128)(2,1)} %grad_ref.1) | copy-start | bytes 3145732
  7.0 39.8 %all-to-all-start = ((s32[32,1,256]{2,1,0:T(1,128)}), s32[32,1,256]{2,1,0:T(1,128)S(1)}, u32[]{:S(2)}, u32[]{:S(2)}) async-start(s32[32,1,256]{2,1,0:T(1,128)} %bitcast.5), calls=%async_computation | async-start | bytes 65536 | tf_op jit(solution)/shard_map/all_to_all | solution.py:380
  17.9 1.2 %copy-start.6 = (bf16[16,256,128]{2,1,0:T(8,128)(2,1)S(1)}, bf16[16,256,128]{2,1,0:T(8,128)(2,1)}, u32[]{:S(2)}) copy-start(bf16[16,256,128]{2,1,0:T(8,128)(2,1)} %start_ref.1) | copy-start | bytes 3145732
  45.6 1.3 %copy-start = (bf16[8192,128]{1,0:T(8,128)(2,1)}, bf16[8192,128]{1,0:T(8,128)(2,1)S(1)}, u32[]{:S(2)}) copy-start(bf16[8192,128]{1,0:T(8,128)(2,1)S(1)} %shard_map.106) | copy-start | bytes 6291460
  46.9 53.5 %all-to-all-start.1 = ((bf16[32,256,128]{2,1,0:T(8,128)(2,1)}), bf16[32,256,128]{2,1,0:T(8,128)(2,1)}, u32[]{:S(2)}, u32[]{:S(2)}) async-start(bf16[32,256,128]{2,1,0:T(8,128)(2,1)} %bitcast.33), calls=%async_computation.1 | async-start | bytes 4194304 | tf_op jit(solution)/shard_map/all_to_all | solution.py:381

commit v2 on v1

--- a/solution.py
+++ b/solution.py
@@ -259,7 +259,7 @@
     )(grad, start, weight, blocks)
 
 
-def table_kernel(front_ref, cell_ref, pos_ref, place_ref, cells_ref, spots_ref, sums_ref):
+def table_kernel(owned, front_ref, cell_ref, pos_ref, place_ref, cells_ref, spots_ref, sums_ref):
     count, capacity = cells_ref.shape
     total = front_ref.shape[1]
     block = 256
@@ -295,15 +295,23 @@
         )
     part = [sums_ref[n * count : (n + 1) * count, :].astype(jnp.int32) for n in range(4)]
     cells_ref[...] = part[0] * 64 + part[1]
-    spots_ref[...] = part[2] * 16 + part[3] - 1
-
-
-def row_table(row_front, row_cells, row_pos, front_place, capacity):
+    spots = part[2] * 16 + part[3] - 1
+    size_y = spots_ref.shape[0]
+    size_x = count // (size_y * owned)
+    for x in range(size_x):
+        for y in range(size_y):
+            at = (x * size_y + y) * owned
+            spots_ref[y, x * owned : (x + 1) * owned, :] = spots[at : at + owned, :]
+
+
+def row_table(row_front, row_cells, row_pos, front_place, capacity, owned, size_y):
     count = front_place.shape[0]
-    shape = jax.ShapeDtypeStruct((count, capacity), jnp.int32)
     return pl.pallas_call(
-        table_kernel,
-        out_shape=(shape, shape),
+        functools.partial(table_kernel, owned),
+        out_shape=(
+            jax.ShapeDtypeStruct((count, capacity), jnp.int32),
+            jax.ShapeDtypeStruct((size_y, count // size_y, capacity), jnp.int32),
+        ),
         in_specs=[pl.BlockSpec(memory_space=pltpu.VMEM)] * 4,
         out_specs=(pl.BlockSpec(memory_space=pltpu.VMEM),) * 2,
         scratch_shapes=[pltpu.VMEM((4 * count, capacity), jnp.float32)],
@@ -316,31 +324,186 @@
     )
 
 
-def pick_kernel(cells_ref, field_ref, out_ref, held_ref):
-    total = out_ref.shape[0]
-    step = 32
-
-    def some(t, carry):
-        for u in range(step):
-            at = t * step + u
-            held_ref[pl.ds(at, 1), :] = field_ref[pl.ds(cells_ref[at], 1), :]
-        return carry
-
-    lax.fori_loop(0, total // step, some, 0)
-    out_ref[...] = held_ref[...].astype(out_ref.dtype)
-
-
-def pick(cells, field):
-    total, width = cells.shape[0], field.shape[1]
+def route_kernel(
+    size_x,
+    size_y,
+    cells_ref,
+    spots_ref,
+    field_ref,
+    schur_ref,
+    out_ref,
+    held_ref,
+    rows_send_ref,
+    rows_in_ref,
+    spots_in_ref,
+    dense_send_ref,
+    dense_in_ref,
+    own_ref,
+    rows_send_sem,
+    rows_in_sem,
+    spots_send_sem,
+    spots_in_sem,
+    dense_send_sem,
+    dense_in_sem,
+):
+    owned, size, width = out_ref.shape
+    capacity = cells_ref.shape[1]
+    gx, gy = lax.axis_index("gx"), lax.axis_index("gy")
+    barrier = pltpu.get_barrier_semaphore()
+    for u in range(1, size_y):
+        pl.semaphore_signal(
+            barrier, inc=1, device_id=(gx, lax.rem(gy + u, size_y)), device_id_type=MESH
+        )
+    for s in range(1, size_x):
+        pl.semaphore_signal(
+            barrier, inc=1, device_id=(lax.rem(gx + s, size_x), gy), device_id_type=MESH
+        )
+    pl.semaphore_wait(barrier, size_x + size_y - 2)
+
+    order = sorted(range(size_x), key=lambda s: (s == 0, abs(2 * s - size_x)))
+
+    def to_peer(source, target, send_sem, recv_sem, device):
+        return pltpu.make_async_remote_copy(
+            src_ref=source,
+            dst_ref=target,
+            send_sem=send_sem,
+            recv_sem=recv_sem,
+            device_id=device,
+            device_id_type=MESH,
+        )
+
+    def spots_copy(u):
+        peer = lax.rem(gy + u, size_y)
+        return to_peer(
+            spots_ref.at[peer],
+            spots_in_ref.at[u],
+            spots_send_sem.at[u],
+            spots_in_sem.at[u],
+            (gx, peer),
+        )
+
+    def rows_copy(t, u):
+        peer = lax.rem(gy + u, size_y)
+        return to_peer(
+            rows_send_ref.at[t, peer],
+            rows_in_ref.at[t, u],
+            rows_send_sem.at[t, u],
+            rows_in_sem.at[t, u],
+            (gx, peer),
+        )
+
+    def dense_copy(t):
+        s = order[t]
+        return to_peer(
+            dense_send_ref.at[t],
+            dense_in_ref.at[t],
+            dense_send_sem.at[t],
+            dense_in_sem.at[t],
+            (lax.rem(gx + s, size_x), gy),
+        )
+
+    for u in range(1, size_y):
+        spots_copy(u).start()
+
+    def gather(t):
+        first = lax.rem(gx + order[t], size_x) * (size_y * owned)
+
+        def one_front(q, carry):
+            base = pl.multiple_of(q * capacity, capacity)
+            for r in range(capacity):
+                cell = cells_ref[first + q, r]
+                held_ref[pl.ds(base + r, 1), :] = field_ref[pl.ds(cell, 1), :]
+            return carry
+
+        lax.fori_loop(0, size_y * owned, one_front, 0)
+        depth = owned * capacity
+        for y in range(size_y):
+            rows_send_ref[t, y] = held_ref[y * depth : (y + 1) * depth, :].astype(jnp.bfloat16)
+        for u in range(1, size_y):
+            rows_copy(t, u).start()
+
+    def assemble(t):
+        plane = lax.rem(gx + order[t], size_x)
+        if t == 0:
+            for u in range(1, size_y):
+                spots_copy(u).wait_recv()
+        for u in range(1, size_y):
+            rows_copy(t, u).wait_recv()
+        positions = lax.broadcasted_iota(jnp.int32, (size, capacity), 0)
+        for o in range(owned):
+            line = pl.ds(plane * owned + o, 1)
+            part = pl.ds(o * capacity, capacity)
+            selectors, sources = [], []
+            for u in range(size_y):
+                spot = spots_ref[gy, line, :] if u == 0 else spots_in_ref[u, line, :]
+                selectors.append(jnp.where(positions == spot, 1.0, 0.0).astype(jnp.bfloat16))
+                sources.append(rows_send_ref[t, gy, part, :] if u == 0 else rows_in_ref[t, u, part, :])
+            if capacity % 128 == 0:
+                selectors = [jnp.concatenate(selectors, axis=1)]
+                sources = [jnp.concatenate(sources, axis=0)]
+            total = jnp.zeros((size, width), jnp.float32)
+            for selector, source in zip(selectors, sources):
+                total = total + jnp.dot(selector, source, preferred_element_type=jnp.float32)
+            if order[t]:
+                dense_send_ref[t, o] = total.astype(jnp.bfloat16)
+            else:
+                own_ref[o] = total
+        if order[t]:
+            dense_copy(t).start()
+
+    gather(0)
+    for t in range(1, size_x):
+        gather(t)
+        assemble(t - 1)
+    assemble(size_x - 1)
+
+    for t in range(size_x - 1):
+        dense_copy(t).wait_recv()
+    for o in range(owned):
+        total = own_ref[o]
+        for t in range(size_x - 1):
+            total = total + dense_in_ref[t, o].astype(jnp.float32)
+        out_ref[o] = jnp.dot(
+            schur_ref[o], total.astype(jnp.bfloat16), preferred_element_type=jnp.float32
+        )
+
+    for u in range(1, size_y):
+        spots_copy(u).wait_send()
+        for t in range(size_x):
+            rows_copy(t, u).wait_send()
+    for t in range(size_x - 1):
+        dense_copy(t).wait_send()
+
+
+def route(cells, spots, field, schur, size_x, size_y):
+    owned, size, _ = schur.shape
+    capacity, width = cells.shape[1], field.shape[1]
     vmem = pl.BlockSpec(memory_space=pltpu.VMEM)
+    dma = pltpu.SemaphoreType.DMA
     return pl.pallas_call(
-        pick_kernel,
-        out_shape=jax.ShapeDtypeStruct((total, width), jnp.bfloat16),
-        in_specs=[pl.BlockSpec(memory_space=pltpu.SMEM), vmem],
+        functools.partial(route_kernel, size_x, size_y),
+        out_shape=jax.ShapeDtypeStruct((owned, size, width), jnp.float32),
+        in_specs=[pl.BlockSpec(memory_space=pltpu.SMEM), vmem, vmem, vmem],
         out_specs=vmem,
-        scratch_shapes=[pltpu.VMEM((total, width), jnp.float32)],
-        compiler_params=pltpu.CompilerParams(vmem_limit_bytes=32 * 1024 * 1024),
-    )(cells, field)
+        scratch_shapes=[
+            pltpu.VMEM((size_y * owned * capacity, width), jnp.float32),
+            pltpu.VMEM((size_x, size_y, owned * capacity, width), jnp.bfloat16),
+            pltpu.VMEM((size_x, size_y, owned * capacity, width), jnp.bfloat16),
+            pltpu.VMEM(spots.shape, jnp.int32),
+            pltpu.VMEM((size_x - 1, owned, size, width), jnp.bfloat16),
+            pltpu.VMEM((size_x - 1, owned, size, width), jnp.bfloat16),
+            pltpu.VMEM((owned, size, width), jnp.float32),
+            dma((size_x, size_y)),
+            dma((size_x, size_y)),
+            dma((size_y,)),
+            dma((size_y,)),
+            dma((size_x - 1,)),
+            dma((size_x - 1,)),
+        ],
+        compiler_params=pltpu.CompilerParams(
+            collective_id=1, has_side_effects=True, vmem_limit_bytes=48 * 1024 * 1024
+        ),
+    )(cells, spots, field, schur)
 
 
 def local(
@@ -363,34 +526,15 @@
     blocks = (same[None, :, None, :, None] * stiffness[:, None, :, None, :]).reshape(
         9, width, width
     )
+    capacity = 2 * row_cells.shape[0] // front_place.shape[0]
+    cells, spots = row_table(
+        row_front, row_cells, row_pos, front_place, capacity, schur.shape[0], size_y
+    )
     adjoint = relax(
         objective_grad, adjoint_start, cell_weight(levels).T, blocks, size_x, size_y
     )
-
-    front_count = front_place.shape[0]
-    devices = size_x * size_y
-    owned, front_size = schur.shape[0], schur.shape[1]
-    capacity = 2 * row_cells.shape[0] // front_count
-    cells, spots = row_table(row_front, row_cells, row_pos, front_place, capacity)
-    rows_out = pick(cells.reshape(-1), adjoint.reshape(rows * cols, width))
-    slot_total = owned * capacity
-    spread = functools.partial(
-        lax.all_to_all, axis_name=("gx", "gy"), split_axis=0, concat_axis=0, tiled=True
-    )
-    spots_in = spread(spots.reshape(devices, slot_total)).reshape(devices, owned, capacity)
-    rows_in = spread(rows_out.reshape(devices, slot_total, width))
-    rows_in = rows_in.reshape(devices, owned, capacity, width)
-    results = []
-    for slot in range(owned):
-        slot_rows = rows_in[:, slot].reshape(devices * capacity, width)
-        slot_spots = spots_in[:, slot].reshape(devices * capacity)
-        selector = (
-            jnp.arange(front_size, dtype=jnp.int32)[:, None] == slot_spots[None, :]
-        ).astype(jnp.bfloat16)
-        assembled = jnp.dot(selector, slot_rows, preferred_element_type=jnp.float32)
-        assembled = assembled.astype(jnp.bfloat16)
-        results.append(jnp.dot(schur[slot], assembled, preferred_element_type=jnp.float32))
-    return (adjoint, jnp.stack(results))
+    field = adjoint.reshape(rows * cols, width)
+    return (adjoint, route(cells, spots, field, schur, size_x, size_y))
 
 
 def solution(mesh):

time: 114 us -> 71.9 us (0.63)
  waiting for transfers between devices: 48.8 us -> 0 us
  Pallas kernels: 30 us -> 62.1 us
  starting transfers between devices: 11.9 us -> 0 us
  matrix products: 6.74 us -> 0 us
  local copies, waits for them, and re-layouts: 12.5 us -> 6.94 us
    all_to_all x2 -> x0, waiting for transfers between devices: 48.8 us -> none  [the longest x1 48.8 us: local(): rows_in = spread(rows_out.reshape(devices, slot_total, width))]
    pallas_call x2, Pallas kernels: 12.4 us -> 43.1 us  [the longest x1 40.1 us: route(): pl.pallas_call(functools.partial(route_kernel, size_x, size_y), out_shape...]
    all_to_all x2 -> x0, starting transfers between devices: 11.9 us -> none  [the longest x1 7.3 us: local(): spread(spots.reshape(devices, slot_total)).reshape(devices, owned, capacity)]
    dot_general x2 -> x0, matrix products: 6.74 us -> none  [local(): jnp.dot(schur[slot], assembled, preferred_element_type=jnp.float32)]
    slice x2 -> x0, local copies, waits for them, and re-layouts: 2.79 us -> none  [the longest x1 2.77 us: local(): slot_rows = rows_in[:, slot].reshape(devices * capacity, width)]
    unnamed x16, local copies, waits for them, and re-layouts: 7.65 us -> 4.93 us
    pallas_call x1, Pallas kernels: 17.6 us -> 19 us  [relax(): pl.pallas_call(functools.partial(relax_kernel, size_x, size_y), out_shape...]
  transfers between devices with their start and end apart: 2 -> 0, of which waited for: 1 -> 0; matrix products, arithmetic and copies ran while one was open for 3% -> 0% of each run, Pallas kernels for 23% -> 0%
where the time goes in v2:
time: 71.9 us; the launch traced here: 71.3 us
  Pallas kernels  62.1 us (86%)
  local copies, waits for them, and re-layouts  6.94 us (10%)
  other arithmetic  1.49 us (2%)
  between operations  0.74 us (1%)
    pallas_call x1, Pallas kernels, route(): pl.pallas_call(functools.partial(route_kernel, size_x, size_y), out_shape...  40.1 us
    pallas_call x1, Pallas kernels, relax(): pl.pallas_call(functools.partial(relax_kernel, size_x, size_y), out_shape...  19 us
    unnamed x16, local copies, waits for them, and re-layouts  4.93 us
    pallas_call x1, Pallas kernels, row_table(): pl.pallas_call(functools.partial(table_kernel, owned), out_shape=(jax.Sha...  2.97 us
    mul x4, local copies, waits for them, and re-layouts, local(): same[None, :, None, :, None] * stiffness[:, None, :, None, :]  1.81 us

profile of v2, /device:TPU:0, one launch (start us, length us, event | category | flops | bytes accessed | tf_op | source)
XLA Modules:
  0.0 71.3 jit_solution(18124794825429990208)
XLA Ops:
  0.6 0.7 %broadcast_multiply_fusion.1 = f32[16,256]{1,0:T(8,128)S(1)} fusion(s32[16,256]{1,0:T(8,128)} %param.11), kind=kLoop, calls=%fused_computation.4 | loop fusion | flops 8192 | bytes 32768 | tf_op jit(solution)/shard_map/mul | solution.py:22
  1.4 0.7 %convert_element_type.10 = f32[16,256]{1,0:T(8,128)S(1)} convert(s32[16,256]{1,0:T(8,128)} %param.11) | non-fusion elementwise | flops 4096 | bytes 32768 | tf_op jit(solution)/shard_map/convert_element_type | solution.py:21
  2.1 0.1 mul.36
  2.2 0.1 mul.37
  2.3 0.0 copy-start.1
  2.3 0.7 copy-done.1
  3.0 0.0 copy-start.2
  3.0 0.7 %copy-done.2 = s32[4096]{0:T(1024)S(1)} copy-done((s32[4096]{0:T(1024)S(1)}, s32[4096]{0:T(1024)}, u32[]{:S(2)}) %copy-start.2) | copy-done | bytes 16408
  3.7 0.0 copy-start.3
  3.7 0.7 %copy-done.3 = s32[4096]{0:T(1024)S(1)} copy-done((s32[4096]{0:T(1024)S(1)}, s32[4096]{0:T(1024)}, u32[]{:S(2)}) %copy-start.3) | copy-done | bytes 16408
  4.4 0.0 copy-start.4
  4.5 0.7 copy-done.4
  5.1 0.0 copy-start.5
  5.1 0.0 copy-start.6
  5.1 3.0 %shard_map.105 = (s32[64,128]{1,0:T(8,128)S(1)}, s32[8,8,128]{2,1,0:T(8,128)S(1)}) custom-call(s32[1,4096]{1,0:T(1,128)S(1)} %bitcast.8, s32[1,4096]{1,0:T(1,128)S(1)} %bitcast.9, s32[1,4096]{1,0:T(1,128)S(1)} %bitcast.10, s32[1,64]{1,0:T(1,128)S(1)} %bitcast.11), custom_call_target="tpu_custom_call" | custom-call | tf_op jit(solution)/shard_map/pallas_call | solution.py:309
  8.1 0.1 copy.13
  8.2 0.1 copy.14
  8.3 1.3 %mul.39 = bf16[9,2,64,2,64]{4,3,2,1,0:T(2,128)(2,1)S(1)} broadcast(bf16[9,64,64]{2,1,0:T(8,128)(2,1)} %param.12), dimensions={0,2,4} | broadcast | bytes 368640 | tf_op jit(solution)/shard_map/mul | solution.py:526
  9.7 0.3 mul.40
  10.0 0.0 copy-done.5
  10.0 0.0 copy-done.6
  10.0 0.0 copy-start
  10.0 19.0 %shard_map.104 = f32[16,256,128]{2,1,0:T(8,128)S(1)} custom-call(bf16[16,256,128]{2,1,0:T(8,128)(2,1)S(1)} %copy-done.5, bf16[16,256,128]{2,1,0:T(8,128)(2,1)S(1)} %copy-done.6, f32[256,16]{1,0:T(8,128)S(1)} %fusion.1.weight_ref, bf16[9,128,128]{2,1,0:T(8,128)(2,1)S(1)} %broadcast_multiply_fusion.blocks_ref), custom_call_target="tpu_custom_call" | custom-call | flops 7247757312 | bytes 4194304 | tf_op jit(solution)/shard_map/pallas_call | solution.py:234
  29.0 0.0 copy-done
  29.0 40.1 %shard_map.106 = f32[2,512,128]{2,1,0:T(8,128)S(1)} custom-call(s32[64,128]{1,0:T(8,128)S(1)} %get-tuple-element.4.cells_ref, s32[8,8,128]{2,1,0:T(8,128)S(1)} %get-tuple-element.5.spots_ref, f32[4096,128]{1,0:T(8,128)S(1)} %bitcast.7, bf16[2,512,512]{2,1,0:T(8,128)(2,1)S(1)} %copy-done), custom_call_target="tpu_custom_call" | custom-call | tf_op jit(solution)/shard_map/pallas_call | solution.py:483
  69.2 1.3 %copy.17 = f32[16,256,128]{2,1,0:T(8,128)} copy(f32[16,256,128]{2,1,0:T(8,128)S(1)} %shard_map.104) | data formatting | bytes 4194304
  70.5 0.8 %copy.18 = f32[2,512,128]{2,1,0:T(8,128)} copy(f32[2,512,128]{2,1,0:T(8,128)S(1)} %shard_map.106) | data formatting | bytes 1048576
  (3 shorter events, 0.1 us)
Async XLA Ops:
  2.3 0.7 %copy-start.1 = (s32[4096,1]{0,1:T(1,128)S(1)}, s32[4096,1]{0,1:T(1,128)}, u32[]{:S(2)}) copy-start(s32[4096,1]{0,1:T(1,128)} %param.14) | copy-start | bytes 49156
  3.0 0.7 %copy-start.2 = (s32[4096]{0:T(1024)S(1)}, s32[4096]{0:T(1024)}, u32[]{:S(2)}) copy-start(s32[4096]{0:T(1024)} %param.13) | copy-start | bytes 49156
  3.7 0.7 %copy-start.3 = (s32[4096]{0:T(1024)S(1)}, s32[4096]{0:T(1024)}, u32[]{:S(2)}) copy-start(s32[4096]{0:T(1024)} %param.15) | copy-start | bytes 49156
  4.4 0.7 copy-start.4
  5.1 4.9 %copy-start.5 = (bf16[16,256,128]{2,1,0:T(8,128)(2,1)S(1)}, bf16[16,256,128]{2,1,0:T(8,128)(2,1)}, u32[]{:S(2)}) copy-start(bf16[16,256,128]{2,1,0:T(8,128)(2,1)} %grad_ref.1) | copy-start | bytes 3145732
  5.1 4.9 %copy-start.6 = (bf16[16,256,128]{2,1,0:T(8,128)(2,1)S(1)}, bf16[16,256,128]{2,1,0:T(8,128)(2,1)}, u32[]{:S(2)}) copy-start(bf16[16,256,128]{2,1,0:T(8,128)(2,1)} %start_ref.1) | copy-start | bytes 3145732
  10.0 19.0 %copy-start = (bf16[2,512,512]{2,1,0:T(8,128)(2,1)S(1)}, bf16[2,512,512]{2,1,0:T(8,128)(2,1)}, u32[]{:S(2)}) copy-start(bf16[2,512,512]{2,1,0:T(8,128)(2,1)} %schur_ref.1) | copy-start | bytes 3145732

commit v3 on v2

--- a/solution.py
+++ b/solution.py
@@ -22,14 +22,15 @@
     return soft_floor + (1.0 - soft_floor) * ratio * ratio * ratio
 
 
-def relax_kernel(
+def relax_part(
     size_x,
     size_y,
     grad_ref,
-    start_ref,
-    weight_ref,
+    levels_ref,
+    stiffness_ref,
     blocks_ref,
     lam_ref,
+    start_ref,
     wide_ref,
     shifted_ref,
     line_ref,
@@ -40,6 +41,7 @@
     col_in_ref,
     send_sem,
     recv_sem,
+    incoming,
 ):
     rows, cols, width = grad_ref.shape
     gx, gy = lax.axis_index("gx"), lax.axis_index("gy")
@@ -60,17 +62,36 @@
     col_in_ref[...] = jnp.zeros_like(col_in_ref)
 
     barrier = pltpu.get_barrier_semaphore()
-    for side in SIDES:
+    for side in SIDES[4:]:
 
         @pl.when(exists(side))
         def _(side=side):
             pl.semaphore_signal(barrier, inc=1, device_id=place(side), device_id_type=MESH)
+
+    for u in range(1, size_y):
+        pl.semaphore_signal(
+            barrier, inc=1, device_id=(gx, lax.rem(gy + u, size_y)), device_id_type=MESH
+        )
+    for u in range(1, size_x):
+        pl.semaphore_signal(
+            barrier, inc=1, device_id=(lax.rem(gx + u, size_x), gy), device_id_type=MESH
+        )
 
     for b in range(3):
         shifted_ref[b, 0] = jnp.zeros((cols, width), jnp.bfloat16)
         shifted_ref[b, rows + 1] = jnp.zeros((cols, width), jnp.bfloat16)
     line_ref[0:8, :] = jnp.zeros((8, width), jnp.float32)
     line_ref[8 + cols : 16 + cols, :] = jnp.zeros((8, width), jnp.float32)
+
+    incoming("stiffness")
+    freedom = stiffness_ref.shape[1]
+    blocks_ref[...] = jnp.zeros_like(blocks_ref)
+    for n in range(9):
+        block = stiffness_ref[n]
+        empty = jnp.zeros((freedom, freedom), jnp.bfloat16)
+        for c in range(width // freedom):
+            parts = [block if e == c else empty for e in range(width // freedom)]
+            blocks_ref[n, c * freedom : (c + 1) * freedom, :] = jnp.concatenate(parts, axis=1)
 
     for i in range(4):
         for b in range(3):
@@ -82,18 +103,25 @@
                 else:
                     big_ref[at] = jnp.zeros((width, width), jnp.bfloat16)
 
+    incoming("levels")
+    weight = cell_weight(levels_ref[...]).T
     for r in range(rows):
-        wide_ref[r] = jnp.broadcast_to(weight_ref[:, r : r + 1], (cols, width))
+        wide_ref[r] = jnp.broadcast_to(weight[:, r : r + 1], (cols, width))
+
+    def line_of(r):
+        return pl.ds(pl.multiple_of(r * cols, cols), cols)
+
+    incoming("start")
 
     def take_start(r, carry):
-        lam_ref[r] = start_ref[r].astype(jnp.float32)
+        lam_ref[line_of(r), :] = start_ref[r].astype(jnp.float32)
         return carry
 
     lax.fori_loop(0, rows, take_start, 0)
 
-    near_x = 1 + jnp.minimum(gx, 1) + jnp.minimum(size_x - 1 - gx, 1)
-    near_y = 1 + jnp.minimum(gy, 1) + jnp.minimum(size_y - 1 - gy, 1)
-    pl.semaphore_wait(barrier, near_x * near_y - 1)
+    near_x = jnp.minimum(gx, 1) + jnp.minimum(size_x - 1 - gx, 1)
+    near_y = jnp.minimum(gy, 1) + jnp.minimum(size_y - 1 - gy, 1)
+    pl.semaphore_wait(barrier, near_x * near_y + size_x + size_y - 2)
 
     def copies(step):
         made = []
@@ -132,7 +160,7 @@
     for step in range(PASSES):
 
         def produce(r, carry):
-            scaled = wide_ref[r] * lam_ref[r]
+            scaled = wide_ref[r] * lam_ref[line_of(r), :]
             line_ref[8 : 8 + cols, :] = scaled
             left, middle, right = spread()
             shifted_ref[0, r + 1] = left
@@ -151,6 +179,9 @@
             @pl.when(exists(side))
             def _(copy=copy):
                 copy.start()
+
+        if step == 0:
+            incoming("grad")
 
         def interior(t, carry):
             r = 4 * t
@@ -168,7 +199,8 @@
                 for j in range(2):
                     at = r + 2 * p + j
                     part = image[p * cols : (p + 1) * cols, j * width : (j + 1) * width]
-                    lam_ref[at] = lam_ref[at] + relax_rate * (
+                    line = line_of(at)
+                    lam_ref[line, :] = lam_ref[line, :] + relax_rate * (
                         grad_ref[at].astype(jnp.float32) - part
                     )
             return carry
@@ -205,8 +237,8 @@
                 else big_ref[3 * depth : 4 * depth, width : 2 * width]
             )
             more = jnp.dot(lhs, piece, preferred_element_type=jnp.float32)
-            at = 0 if end == 0 else rows - 1
-            lam_ref[at] = lam_ref[at] - relax_rate * more
+            line = line_of(0 if end == 0 else rows - 1)
+            lam_ref[line, :] = lam_ref[line, :] - relax_rate * more
 
         for end in range(2):
             edge_ref[end, 8 : 8 + rows, :] = col_in_ref[step, end].astype(jnp.float32)
@@ -223,43 +255,11 @@
                 )
             at = 0 if end == 0 else cols - 1
             for r in range(rows):
-                lam_ref[r, at : at + 1, :] = (
-                    lam_ref[r, at : at + 1, :] - relax_rate * more[r : r + 1, :]
-                )
-
-
-def relax(grad, start, weight, blocks, size_x, size_y):
-    rows, cols, width = grad.shape
-    vmem = pl.BlockSpec(memory_space=pltpu.VMEM)
-    return pl.pallas_call(
-        functools.partial(relax_kernel, size_x, size_y),
-        out_shape=jax.ShapeDtypeStruct((rows, cols, width), jnp.float32),
-        in_specs=[vmem] * 4,
-        out_specs=vmem,
-        scratch_shapes=[
-            pltpu.VMEM((rows, cols, width), jnp.float32),
-            pltpu.VMEM((3, rows + 2, cols, width), jnp.bfloat16),
-            pltpu.VMEM((cols + 16, width), jnp.float32),
-            pltpu.VMEM((12 * width, 2 * width), jnp.bfloat16),
-            pltpu.VMEM((2, rows + 16, width), jnp.float32),
-            pltpu.VMEM((2, rows, width), jnp.bfloat16),
-            pltpu.VMEM((PASSES, 2, cols, width), jnp.bfloat16),
-            pltpu.VMEM((PASSES, 6, rows, width), jnp.bfloat16),
-            pltpu.SemaphoreType.DMA((PASSES, 8)),
-            pltpu.SemaphoreType.DMA((PASSES, 8)),
-        ],
-        compiler_params=pltpu.CompilerParams(
-            collective_id=0, has_side_effects=True, vmem_limit_bytes=48 * 1024 * 1024
-        ),
-        cost_estimate=pl.CostEstimate(
-            flops=6 * 2 * rows * cols * width * 9 * width,
-            bytes_accessed=8 * rows * cols * width,
-            transcendentals=0,
-        ),
-    )(grad, start, weight, blocks)
-
-
-def table_kernel(owned, front_ref, cell_ref, pos_ref, place_ref, cells_ref, spots_ref, sums_ref):
+                cell = slice(r * cols + at, r * cols + at + 1)
+                lam_ref[cell, :] = lam_ref[cell, :] - relax_rate * more[r : r + 1, :]
+
+
+def table_part(owned, front_ref, cell_ref, pos_ref, place_ref, cells_ref, spots_ref, sums_ref):
     count, capacity = cells_ref.shape
     total = front_ref.shape[1]
     block = 256
@@ -304,27 +304,7 @@
             spots_ref[y, x * owned : (x + 1) * owned, :] = spots[at : at + owned, :]
 
 
-def row_table(row_front, row_cells, row_pos, front_place, capacity, owned, size_y):
-    count = front_place.shape[0]
-    return pl.pallas_call(
-        functools.partial(table_kernel, owned),
-        out_shape=(
-            jax.ShapeDtypeStruct((count, capacity), jnp.int32),
-            jax.ShapeDtypeStruct((size_y, count // size_y, capacity), jnp.int32),
-        ),
-        in_specs=[pl.BlockSpec(memory_space=pltpu.VMEM)] * 4,
-        out_specs=(pl.BlockSpec(memory_space=pltpu.VMEM),) * 2,
-        scratch_shapes=[pltpu.VMEM((4 * count, capacity), jnp.float32)],
-        compiler_params=pltpu.CompilerParams(vmem_limit_bytes=32 * 1024 * 1024),
-    )(
-        row_front.reshape(1, -1),
-        row_cells.reshape(1, -1),
-        row_pos.reshape(1, -1),
-        front_place.reshape(1, -1),
-    )
-
-
-def route_kernel(
+def route_part(
     size_x,
     size_y,
     cells_ref,
@@ -349,17 +329,6 @@
     owned, size, width = out_ref.shape
     capacity = cells_ref.shape[1]
     gx, gy = lax.axis_index("gx"), lax.axis_index("gy")
-    barrier = pltpu.get_barrier_semaphore()
-    for u in range(1, size_y):
-        pl.semaphore_signal(
-            barrier, inc=1, device_id=(gx, lax.rem(gy + u, size_y)), device_id_type=MESH
-        )
-    for s in range(1, size_x):
-        pl.semaphore_signal(
-            barrier, inc=1, device_id=(lax.rem(gx + s, size_x), gy), device_id_type=MESH
-        )
-    pl.semaphore_wait(barrier, size_x + size_y - 2)
-
     order = sorted(range(size_x), key=lambda s: (s == 0, abs(2 * s - size_x)))
 
     def to_peer(source, target, send_sem, recv_sem, device):
@@ -475,17 +444,130 @@
         dense_copy(t).wait_send()
 
 
-def route(cells, spots, field, schur, size_x, size_y):
+NAMES = ("grad", "start", "levels", "stiffness", "schur")
+
+
+def table_kernel(owned, *refs):
+    given, (cells_ref, spots_ref), held = refs[:4], refs[4:6], refs[6:10]
+    sums_ref, in_sem = refs[10:]
+    copies = [
+        pltpu.make_async_copy(source, target, in_sem.at[n])
+        for n, (source, target) in enumerate(zip(given, held))
+    ]
+    for copy in copies:
+        copy.start()
+    for copy in copies:
+        copy.wait()
+    table_part(owned, *held, cells_ref, spots_ref, sums_ref)
+
+
+def row_table(given, capacity, owned, size_y):
+    count = given[3].shape[1]
+    return pl.pallas_call(
+        functools.partial(table_kernel, owned),
+        out_shape=(
+            jax.ShapeDtypeStruct((count, capacity), jnp.int32),
+            jax.ShapeDtypeStruct((size_y, count // size_y, capacity), jnp.int32),
+        ),
+        in_specs=[pl.BlockSpec(memory_space=pl.ANY)] * 4,
+        out_specs=(pl.BlockSpec(memory_space=pltpu.VMEM),) * 2,
+        scratch_shapes=[
+            *[pltpu.VMEM(x.shape, x.dtype) for x in given],
+            pltpu.VMEM((4 * count, capacity), jnp.float32),
+            pltpu.SemaphoreType.DMA((4,)),
+        ],
+        compiler_params=pltpu.CompilerParams(vmem_limit_bytes=60 * 1024 * 1024),
+    )(*given)
+
+
+def whole_kernel(size_x, size_y, *refs):
+    count = len(NAMES)
+    given = dict(zip(NAMES, refs[:count]))
+    cells_ref, spots_ref, lam_ref, out_ref = refs[count : count + 4]
+    held = dict(zip(NAMES, refs[count + 4 : 2 * count + 4]))
+    in_sem, blocks_ref = refs[2 * count + 4 : 2 * count + 6]
+    relax_refs = refs[2 * count + 6 : 2 * count + 16]
+    route_refs = refs[2 * count + 16 :]
+
+    def copy_in(name):
+        return pltpu.make_async_copy(given[name], held[name], in_sem.at[NAMES.index(name)])
+
+    for name in ("stiffness", "levels", "start", "grad", "schur"):
+        copy_in(name).start()
+
+    def incoming(name):
+        copy_in(name).wait()
+
+    relax_part(
+        size_x,
+        size_y,
+        held["grad"],
+        held["levels"],
+        held["stiffness"],
+        blocks_ref,
+        lam_ref,
+        held["start"],
+        *relax_refs,
+        incoming,
+    )
+    incoming("schur")
+    route_part(
+        size_x,
+        size_y,
+        cells_ref,
+        spots_ref,
+        lam_ref,
+        held["schur"],
+        out_ref,
+        *route_refs,
+    )
+
+
+def local(
+    size_x,
+    size_y,
+    objective_grad,
+    adjoint_start,
+    levels,
+    stiffness,
+    row_cells,
+    row_front,
+    row_pos,
+    front_place,
+    schur,
+):
+    rows, cols, width = objective_grad.shape
     owned, size, _ = schur.shape
-    capacity, width = cells.shape[1], field.shape[1]
+    count = front_place.shape[0]
+    capacity = 2 * row_cells.shape[0] // count
+    listed = [x.reshape(1, -1) for x in (row_front, row_cells, row_pos, front_place)]
+    cells, spots = row_table(listed, capacity, owned, size_y)
+    given = (objective_grad, adjoint_start, levels, stiffness, schur)
     vmem = pl.BlockSpec(memory_space=pltpu.VMEM)
     dma = pltpu.SemaphoreType.DMA
-    return pl.pallas_call(
-        functools.partial(route_kernel, size_x, size_y),
-        out_shape=jax.ShapeDtypeStruct((owned, size, width), jnp.float32),
-        in_specs=[pl.BlockSpec(memory_space=pltpu.SMEM), vmem, vmem, vmem],
-        out_specs=vmem,
+    adjoint, values = pl.pallas_call(
+        functools.partial(whole_kernel, size_x, size_y),
+        out_shape=(
+            jax.ShapeDtypeStruct((rows * cols, width), jnp.float32),
+            jax.ShapeDtypeStruct((owned, size, width), jnp.float32),
+        ),
+        in_specs=[pl.BlockSpec(memory_space=pl.ANY)] * len(given)
+        + [pl.BlockSpec(memory_space=pltpu.SMEM), vmem],
+        out_specs=(vmem, vmem),
         scratch_shapes=[
+            *[pltpu.VMEM(x.shape, x.dtype) for x in given],
+            dma((len(given),)),
+            pltpu.VMEM((9, width, width), jnp.bfloat16),
+            pltpu.VMEM((rows, cols, width), jnp.float32),
+            pltpu.VMEM((3, rows + 2, cols, width), jnp.bfloat16),
+            pltpu.VMEM((cols + 16, width), jnp.float32),
+            pltpu.VMEM((12 * width, 2 * width), jnp.bfloat16),
+            pltpu.VMEM((2, rows + 16, width), jnp.float32),
+            pltpu.VMEM((2, rows, width), jnp.bfloat16),
+            pltpu.VMEM((PASSES, 2, cols, width), jnp.bfloat16),
+            pltpu.VMEM((PASSES, 6, rows, width), jnp.bfloat16),
+            dma((PASSES, 8)),
+            dma((PASSES, 8)),
             pltpu.VMEM((size_y * owned * capacity, width), jnp.float32),
             pltpu.VMEM((size_x, size_y, owned * capacity, width), jnp.bfloat16),
             pltpu.VMEM((size_x, size_y, owned * capacity, width), jnp.bfloat16),
@@ -501,40 +583,10 @@
             dma((size_x - 1,)),
         ],
         compiler_params=pltpu.CompilerParams(
-            collective_id=1, has_side_effects=True, vmem_limit_bytes=48 * 1024 * 1024
+            collective_id=0, has_side_effects=True, vmem_limit_bytes=56 * 1024 * 1024
         ),
-    )(cells, spots, field, schur)
-
-
-def local(
-    size_x,
-    size_y,
-    objective_grad,
-    adjoint_start,
-    levels,
-    stiffness,
-    row_cells,
-    row_front,
-    row_pos,
-    front_place,
-    schur,
-):
-    rows, cols, width = objective_grad.shape
-    freedom = stiffness.shape[1]
-    cases = width // freedom
-    same = jnp.eye(cases, dtype=stiffness.dtype)
-    blocks = (same[None, :, None, :, None] * stiffness[:, None, :, None, :]).reshape(
-        9, width, width
-    )
-    capacity = 2 * row_cells.shape[0] // front_place.shape[0]
-    cells, spots = row_table(
-        row_front, row_cells, row_pos, front_place, capacity, schur.shape[0], size_y
-    )
-    adjoint = relax(
-        objective_grad, adjoint_start, cell_weight(levels).T, blocks, size_x, size_y
-    )
-    field = adjoint.reshape(rows * cols, width)
-    return (adjoint, route(cells, spots, field, schur, size_x, size_y))
+    )(*given, cells, spots)
+    return (adjoint.reshape(rows, cols, width), values)
 
 
 def solution(mesh):

time: 71.9 us -> 68.4 us (0.951)
  local copies, waits for them, and re-layouts: 6.94 us -> 3.97 us
  other arithmetic: 1.49 us -> 0 us
  Pallas kernels: 62.1 us -> 63.5 us
    mul x5 -> x0, local copies, waits for them, and re-layouts: 1.91 us -> none  [the longest x4 1.81 us: local(): same[None, :, None, :, None] * stiffness[:, None, :, None, :]]
    pallas_call x1, Pallas kernels: 2.97 us -> 4.38 us  [row_table(): pl.pallas_call(functools.partial(table_kernel, owned), out_shape=(jax.Sha...]
    unnamed x16 -> x4, local copies, waits for them, and re-layouts: 4.93 us -> 3.97 us
    mul x2 -> x0, other arithmetic: 0.75 us -> none  [the longest x1 0.72 us: cell_weight(): return soft_floor + (1.0 - soft_floor) * ratio * ratio * ratio]
    convert_element_type x2 -> x0, other arithmetic: 0.73 us -> none  [the longest x1 0.72 us: cell_weight(): ratio = levels.astype(jnp.float32) / LEVELS]
    pallas_call x2 -> x1, Pallas kernels: 59.1 us -> 59.1 us  [local(): pl.pallas_call(functools.partial(whole_kernel, size_x, size_y), out_shape...]
where the time goes in v3:
time: 68.4 us; the launch traced here: 68.1 us
  Pallas kernels  63.5 us (93%)
  local copies, waits for them, and re-layouts  3.97 us (6%)
    pallas_call x1, Pallas kernels, local(): pl.pallas_call(functools.partial(whole_kernel, size_x, size_y), out_shape...  59.1 us
    pallas_call x1, Pallas kernels, row_table(): pl.pallas_call(functools.partial(table_kernel, owned), out_shape=(jax.Sha...  4.38 us
    unnamed x4, local copies, waits for them, and re-layouts  3.97 us

profile of v3, /device:TPU:0, one launch (start us, length us, event | category | flops | bytes accessed | tf_op | source)
XLA Modules:
  0.0 68.1 jit_solution(338259141525533526)
XLA Ops:
  0.6 4.4 %shard_map.104 = (s32[64,128]{1,0:T(8,128)}, s32[8,8,128]{2,1,0:T(8,128)}) custom-call(s32[1,4096]{1,0:T(1,128)} %bitcast.6, s32[1,4096]{1,0:T(1,128)} %bitcast.7, s32[1,4096]{1,0:T(1,128)} %bitcast.8, s32[1,64]{1,0:T(1,128)} %bitcast.9), custom_call_target="tpu_custom_call" | custom-call | tf_op jit(solution)/shard_map/pallas_call | solution.py:466
  5.0 59.1 %shard_map.105 = (f32[4096,128]{1,0:T(8,128)}, f32[2,512,128]{2,1,0:T(8,128)}) custom-call(bf16[16,256,128]{2,1,0:T(8,128)(2,1)} %refs_0_.1, bf16[16,256,128]{2,1,0:T(8,128)(2,1)} %refs_1_.1, s32[16,256]{1,0:T(8,128)} %refs_2_.1, bf16[9,64,64]{2,1,0:T(8,128)(2,1)} %refs_3_.1, bf16[2,512,512]{2,1,0:T(8,128)(2,1)} %refs_4_.1, ...), custom_call_target="tpu_custom_call" | custom-call | tf_op jit(solution)/shard_map/pallas_call | solution.py:548
  64.1 0.0 copy-start
  64.2 3.2 %copy.13 = f32[16,256,128]{2,1,0:T(8,128)} copy(f32[16,256,128]{2,1,0:T(8,128)} %bitcast.5) | data formatting | bytes 4194304
  67.3 0.0 copy-done
  67.3 0.8 %copy.14 = f32[2,512,128]{2,1,0:T(8,128)} copy(f32[2,512,128]{2,1,0:T(8,128)S(1)} %copy-done) | data formatting | bytes 1048576
Async XLA Ops:
  64.1 3.2 %copy-start = (f32[2,512,128]{2,1,0:T(8,128)S(1)}, f32[2,512,128]{2,1,0:T(8,128)}, u32[]{:S(2)}) copy-start(f32[2,512,128]{2,1,0:T(8,128)} %get-tuple-element.13) | copy-start | bytes 1572868
